TPU v7x, 512 devices: a whole 4x4x16 slice. The times are simulated.
512 devices in a mesh: lon: 64 (over z_hi, x, y, core), lat: 8 (over z_lo).
Axes of the slice: x: 4, y: 4, z: 16 (z_hi: 2, z_lo: 8; z = z_hi * 8 + z_lo), core: 2. Of those that a mesh axis runs over, the one named last changes fastest.
Arguments:
- field: bfloat16 [512, 1152, 512], P('lat', 'lon'), may hold values from -6 to 6
- region: int32 [512, 1152], P('lat', 'lon'), may hold values from 0 to 5, as said below
- w_qkv: bfloat16 [512, 1536], replicated, may hold values from -0.25 to 0.25
- w_proj: bfloat16 [512, 512], replicated, may hold values from -0.25 to 0.25
- w_up: bfloat16 [512, 2048], P(None, 'lat'), may hold values from -0.25 to 0.25
- w_down: bfloat16 [2048, 512], P('lat'), may hold values from -0.125 to 0.125
- position_bias: float32 [16, 72, 72], replicated, may hold values from -6 to 252
Outputs:
- result: bfloat16 [512, 1152, 512], P('lat', 'lon')
Inputs may be any that keep to these rules, and one draw needn't show every extreme that they name: `region`: rows 0 to 3 of the grid carry ids 3 to 5, all other rows ids 0 to 2.
All inputs are finite; a program needn't handle non-finite values.
Results may differ from a plain program's by a relative error of at most 0.0075.
Values may be sent and summed in bfloat16 or wider, within the bound.
A program may use at most 128 MiB of HBM per device.

v0:
```python
import jax
import jax.numpy as jnp
from jax import lax
from jax.sharding import PartitionSpec as P

D = 512
HEADS = 16
HEAD_DIM = 32
WIN_ROWS = 8
WIN_COLS = 9
WIN_TOK = 72
SHIFT = 4


def from_behind(value, axis, steps):
    count = lax.axis_size(axis)
    pairs = [(source, (source + steps) % count) for source in range(count)]
    return lax.ppermute(value, axis, pairs)


def layer_norm(values):
    floats = values.astype(jnp.float32)
    center = jnp.mean(floats, axis=-1, keepdims=True)
    spread = jnp.mean((floats - center) ** 2, axis=-1, keepdims=True)
    return ((floats - center) * lax.rsqrt(spread + 1e-05)).astype(jnp.bfloat16)


def to_windows(block):
    rows, cols = (block.shape[0], block.shape[1])
    shaped = block.reshape(rows // WIN_ROWS, WIN_ROWS, cols // WIN_COLS, WIN_COLS, -1)
    return shaped.transpose(0, 2, 1, 3, 4).reshape(-1, WIN_TOK, block.shape[2])


def from_windows(wins, rows, cols):
    shaped = wins.reshape(rows // WIN_ROWS, cols // WIN_COLS, WIN_ROWS, WIN_COLS, -1)
    return shaped.transpose(0, 2, 1, 3, 4).reshape(rows, cols, -1)


def window_attention(query, keys, vals, marks, position_bias):
    count = query.shape[0]
    query_h = query.reshape(count, WIN_TOK, HEADS, HEAD_DIM)
    keys_h = keys.reshape(count, WIN_TOK, HEADS, HEAD_DIM)
    vals_h = vals.reshape(count, WIN_TOK, HEADS, HEAD_DIM)
    scores = jnp.einsum(
        "wqhd,wkhd->whqk", query_h, keys_h, preferred_element_type=jnp.float32
    ) * HEAD_DIM ** (-0.5)
    scores = scores + position_bias[None]
    same_region = marks[:, :, None] == marks[:, None, :]
    scores = jnp.where(same_region[:, None], scores, jnp.float32(-1e30))
    largest = jnp.max(scores, axis=-1, keepdims=True)
    expo = jnp.exp(scores - largest)
    probs = (expo / jnp.sum(expo, axis=-1, keepdims=True)).astype(jnp.bfloat16)
    outputs = jnp.einsum("whqk,wkhd->wqhd", probs, vals_h, preferred_element_type=jnp.float32)
    return outputs.reshape(count, WIN_TOK, D).astype(jnp.bfloat16)


def roll_in(field, marks):
    below = from_behind((field[:SHIFT], marks[:SHIFT]), "lat", -1)
    field = jnp.concatenate([field[SHIFT:], below[0]], axis=0)
    marks = jnp.concatenate([marks[SHIFT:], below[1]], axis=0)
    beside = from_behind((field[:, :SHIFT], marks[:, :SHIFT]), "lon", -1)
    field = jnp.concatenate([field[:, SHIFT:], beside[0]], axis=1)
    marks = jnp.concatenate([marks[:, SHIFT:], beside[1]], axis=1)
    return (field, marks)


def roll_out(field):
    behind = from_behind(field[:, -SHIFT:], "lon", 1)
    field = jnp.concatenate([behind, field[:, :-SHIFT]], axis=1)
    above = from_behind(field[-SHIFT:], "lat", 1)
    return jnp.concatenate([above, field[:-SHIFT]], axis=0)


def add_rows(left, piece):
    return jnp.dot(left, piece, preferred_element_type=jnp.float32)


def mlp_branch(mixed, w_up, w_down):
    normed2 = layer_norm(mixed)
    inner = jnp.dot(
        normed2, lax.all_gather(w_up, "lat", axis=1, tiled=True), preferred_element_type=jnp.float32
    )
    hidden = jax.nn.gelu(inner, approximate=True).astype(jnp.bfloat16)
    summed = add_rows(hidden, lax.all_gather(w_down, "lat", axis=0, tiled=True))
    return (mixed.astype(jnp.float32) + summed).astype(jnp.bfloat16)


def local(field, region, w_qkv, w_proj, w_up, w_down, position_bias):
    rows, cols = (field.shape[0], field.shape[1])
    width = w_qkv.shape[0]
    shifted, marks = roll_in(field, region.astype(jnp.bfloat16))
    flat = shifted.reshape(-1, width)
    normed = layer_norm(flat)
    qkv = jnp.dot(normed, w_qkv, preferred_element_type=jnp.float32).astype(jnp.bfloat16)
    qkv_win = to_windows(qkv.reshape(rows, cols, 3 * width))
    mark_win = to_windows(marks[:, :, None])[:, :, 0]
    attended = window_attention(
        qkv_win[:, :, :width],
        qkv_win[:, :, width : 2 * width],
        qkv_win[:, :, 2 * width :],
        mark_win,
        position_bias,
    )
    attended = from_windows(attended, rows, cols).reshape(-1, width)
    mixed = (
        flat.astype(jnp.float32) + jnp.dot(attended, w_proj, preferred_element_type=jnp.float32)
    ).astype(jnp.bfloat16)
    output = mlp_branch(mixed, w_up, w_down)
    return roll_out(output.reshape(rows, cols, width))


def solution(mesh):
    placed = (P("lat", "lon", None), P("lat", "lon"), P(), P(), P(None, "lat"), P("lat", None), P())
    return jax.shard_map(
        local, mesh=mesh, in_specs=placed, out_specs=P("lat", "lon", None), check_vma=False
    )
```

profile of v0, /device:TPU:0, one launch (start us, length us, event | category | flops | bytes accessed | tf_op | source)
XLA Modules:
  0.0 217.0 jit_solution(16661687713430117427)
XLA Ops:
  8.2 7.8 %collective-permute-start = (bf16[4,18,512]{2,0,1:T(4,128)(2,1)S(1)}, bf16[4,18,512]{2,0,1:T(4,128)(2,1)S(1)}, u32[]{:S(2)}, u32[]{:S(2)}) collective-permute-start(bf16[4,18,512]{2,0,1:T(4,128)(2,1)S(1)} %slice.46), channel_id=1, source_target_pairs={{0,7},{1,0},{2,1},{3,2},{4,3},{5,4},{6,5},{7,6},{8,15},{9,8},{10,9... | collective-permute-start | bytes 221192 | tf_op jit(solution)/shard_map/ppermute | solution.py:18
  16.8 2.0 collective-permute-start.2
  18.8 1.7 slice.45
  22.3 12.1 %collective-permute-start.3 = (bf16[64,4]{0,1:T(4,128)(2,1)S(1)}, bf16[64,4]{0,1:T(4,128)(2,1)S(1)}, u32[]{:S(2)}, u32[]{:S(2)}) collective-permute-start(bf16[64,4]{0,1:T(4,128)(2,1)S(1)} %pad_maximum_fusion.4), channel_id=1, source_target_pairs={{0,504},{8,0},{16,8},{24,16},{32,24},{40,32},{48,40},{56,48},{64,5... | collective-permute-start | bytes 1544 | tf_op jit(solution)/shard_map/ppermute | solution.py:18
  34.6 1.2 collective-permute-done.3
  36.2 16.5 %collective-permute-start.1 = (bf16[64,4,512]{2,0,1:T(8,128)(2,1)S(1)}, bf16[64,4,512]{2,0,1:T(8,128)(2,1)S(1)}, u32[]{:S(2)}, u32[]{:S(2)}) collective-permute-start(bf16[64,4,512]{2,0,1:T(8,128)(2,1)S(1)} %pad_maximum_fusion.1), channel_id=1, source_target_pairs={{0,504},{8,0},{16,8},{24,16},{32,24},{40,32},{48,40},{56,48},{64,5... | collective-permute-start | bytes 786440 | tf_op jit(solution)/shard_map/ppermute | solution.py:18
  53.6 1.3 fusion.30
  54.9 12.6 %collective-permute-done.1 = bf16[64,4,512]{2,0,1:T(8,128)(2,1)S(1)} collective-permute-done((bf16[64,4,512]{2,0,1:T(8,128)(2,1)S(1)}, bf16[64,4,512]{2,0,1:T(8,128)(2,1)S(1)}, u32[]{:S(2)}, u32[]{:S(2)}) %collective-permute-start.1) | collective-permute-done | bytes 262176 | tf_op jit(solution)/shard_map/ppermute | solution.py:18
  68.9 3.1 %copy.25 = f32[64,18,512]{2,1,0:T(8,128)} copy(f32[64,18,512]{2,0,1:T(8,128)S(1)} %maximum_convert_fusion) | data formatting | bytes 4718592 | tf_op jit(solution)/shard_map/convert_element_type | solution.py:106
  72.0 3.6 %reshape.77 = f32[1152,512]{1,0:T(8,128)} reshape(f32[64,18,512]{2,1,0:T(8,128)} %copy.25) | data formatting | bytes 4718592 | tf_op jit(solution)/shard_map/convert_element_type | solution.py:106
  75.7 5.5 %convolution_convert_fusion = bf16[1152,1536]{1,0:T(8,128)(2,1)} fusion(bf16[512,1536]{1,0:T(8,128)(2,1)S(1)} %copy-done, f32[1152,512]{1,0:T(8,128)} %reshape.77, f32[1152]{0:T(1024)S(1)} %rsqrt.20, f32[1152]{0:T(1024)S(1)} %div.23), kind=kOutput, calls=%fused_computation.13 | convolution fusion | flops 1815478272 | bytes 7480320 | tf_op jit(solution)/shard_map/dot_general | solution.py:94
  81.2 7.3 %reshape_reshape.6 = bf16[8,8,2,9,1536]{4,3,2,1,0:T(8,128)(2,1)} reshape(bf16[1152,1536]{1,0:T(8,128)(2,1)} %convolution_convert_fusion) | data formatting | bytes 7077888 | tf_op jit(solution)/shard_map/reshape;reshape | solution.py:30
  88.5 8.4 %copy.28 = bf16[8,2,8,9,1536]{4,1,0,3,2:T(2,128)(2,1)} copy(bf16[8,2,8,9,1536]{4,3,1,2,0:T(8,128)(2,1)} %bitcast.31) | data formatting | bytes 7077888 | tf_op jit(solution)/shard_map/transpose | solution.py:31
  96.9 8.4 %reshape.72 = bf16[16,72,1536]{2,0,1:T(8,128)(2,1)} reshape(bf16[8,2,8,9,1536]{4,1,0,3,2:T(2,128)(2,1)} %copy.28) | data formatting | bytes 7077888 | tf_op jit(solution)/shard_map/reshape | solution.py:31
  105.3 3.4 %fusion.41 = (bf16[16,72,512]{2,0,1:T(8,128)(2,1)S(1)}, bf16[16,72,512]{2,0,1:T(8,128)(2,1)}, bf16[16,72,512]{2,0,1:T(8,128)(2,1)S(1)}) fusion(bf16[16,72,1536]{2,0,1:T(8,128)(2,1)} %reshape.72), kind=kLoop, calls=%fused_computation.63 | loop fusion | bytes 7077888 | tf_op jit(solution)/shard_map/slice | solution.py:99
  108.6 4.1 %copy.31 = bf16[16,72,512]{1,2,0:T(8,128)(2,1)} copy(bf16[16,72,512]{2,0,1:T(8,128)(2,1)} %get-tuple-element.6) | data formatting | bytes 2359296 | tf_op jit(solution)/shard_map/slice | solution.py:98
  112.7 2.6 %copy.32 = bf16[16,72,512]{1,2,0:T(8,128)(2,1)} copy(bf16[16,72,512]{2,0,1:T(8,128)(2,1)S(1)} %get-tuple-element.5) | data formatting | bytes 2359296 | tf_op jit(solution)/shard_map/slice | solution.py:99
  115.4 2.6 %copy.29 = bf16[16,72,512]{1,2,0:T(8,128)(2,1)} copy(bf16[16,72,512]{2,0,1:T(8,128)(2,1)S(1)} %get-tuple-element.7) | data formatting | bytes 2359296 | tf_op jit(solution)/shard_map/slice | solution.py:100
  118.0 10.3 %fusion.42 = (f32[16,16,72]{2,1,0:T(8,128)S(1)}, f32[16,16,72,72]{2,3,1,0:T(8,128)}) fusion(f32[16,72,72]{1,2,0:T(8,128)S(1)} %copy-done.4, pred[16,72,72]{1,2,0:T(8,128)(4,1)S(1)} %copy-done.6, bf16[16,72,16,32]{1,3,2,0:T(8,128)(2,1)} %bitcast.33, bf16[16,72,16,32]{1,3,2,0:T(8,128)(2,1)} %bitcast.34), kind=kOutput, calls=%fused_computation.64 | convolution fusion | flops 91570248 | bytes 8156160 | tf_op jit(solution)/shard_map/sub | solution.py:51
  128.3 7.1 %convert_bitcast_fusion = bf16[16,72,16,32]{1,3,2,0:T(8,128)(2,1)} fusion(bf16[16,72,16,32]{1,3,2,0:T(8,128)(2,1)} %bitcast.35, f32[16,16,72,72]{2,3,1,0:T(8,128)} %get-tuple-element.9, f32[16,16,72]{2,1,0:T(8,128)S(1)} %get-tuple-element.8), kind=kOutput, calls=%fused_computation.32 | convolution fusion | flops 88178688 | bytes 7741440 | tf_op jit(solution)/shard_map/whqk,wkhd->wqhd/dot_general | solution.py:53
  135.4 6.9 %copy.35 = bf16[16,72,16,32]{3,2,0,1:T(8,128)(2,1)} copy(bf16[16,72,16,32]{1,3,2,0:T(8,128)(2,1)} %convert_bitcast_fusion) | data formatting | bytes 2359296 | tf_op jit(solution)/shard_map/convert_element_type | solution.py:54
  142.3 6.8 %convert_element_type.58 = bf16[8,2,8,9,512]{4,1,0,3,2:T(2,128)(2,1)S(1)} reshape(bf16[16,72,16,32]{3,2,0,1:T(8,128)(2,1)} %copy.35) | data formatting | bytes 2359296 | tf_op jit(solution)/shard_map/convert_element_type | solution.py:54
  149.1 2.7 %copy.36 = bf16[8,8,2,9,512]{4,3,2,1,0:T(8,128)(2,1)} copy(bf16[8,8,2,9,512]{4,2,0,3,1:T(2,128)(2,1)S(1)} %bitcast.32) | data formatting | bytes 2359296 | tf_op jit(solution)/shard_map/transpose | solution.py:36
  151.8 2.8 %reshape_reshape.7 = bf16[1152,512]{1,0:T(8,128)(2,1)S(1)} reshape(bf16[8,8,2,9,512]{4,3,2,1,0:T(8,128)(2,1)} %copy.36) | data formatting | bytes 2359296 | tf_op jit(solution)/shard_map/reshape;reshape | solution.py:104
  154.6 2.5 %convert_reduce_fusion = (f32[1152]{0:T(1024)S(1)}, bf16[1152,512]{1,0:T(8,128)(2,1)S(1)}) fusion(f32[1152,512]{1,0:T(8,128)} %reshape.77, bf16[1152,512]{1,0:T(8,128)(2,1)S(1)} %reshape_reshape.7, bf16[512,512]{1,0:T(8,128)(2,1)S(1)} %copy-done.5), kind=kOutput, calls=%fused_computation.22 | convolution fusion | flops 606337920 | bytes 5247488 | tf_op jit(solution)/shard_map/dot_general | solution.py:106
  157.9 8.7 %fusion.16 = bf16[1152,512]{1,0:T(8,128)(2,1)} fusion(bf16[2048,512]{1,0:T(8,128)(2,1)} %all-gather.5.cloned.1.call-done, bf16[1152,512]{1,0:T(8,128)(2,1)S(1)} %get-tuple-element.11, bf16[512,2048]{1,0:T(8,128)(2,1)} %all-gather.3.cloned.1.call-done, f32[1152]{0:T(1024)S(1)} %add_rsqrt_fusion.1, f32[1152]{0:T(1024)S(1)} %broadcast_multiply_fusion.1), kind=kOutput, calls=%fused_computation.25 | convolution fusion | flops 4857200640 | bytes 6562816 | tf_op jit(solution)/shard_map/dot_general | solution.py:75
  166.6 2.2 %reshape.76 = bf16[64,18,512]{2,1,0:T(8,128)(2,1)S(1)} reshape(bf16[1152,512]{1,0:T(8,128)(2,1)} %fusion.16) | data formatting | bytes 2359296 | tf_op jit(solution)/shard_map/reshape | solution.py:109
  168.9 1.9 collective-permute-start.4
  171.0 23.8 %collective-permute-done.4 = bf16[64,4,512]{2,1,0:T(4,128)(2,1)S(1)} collective-permute-done((bf16[64,4,512]{2,1,0:T(4,128)(2,1)S(1)}, bf16[64,4,512]{2,1,0:T(4,128)(2,1)S(1)}, u32[]{:S(2)}, u32[]{:S(2)}) %collective-permute-start.4) | collective-permute-done | bytes 262176 | tf_op jit(solution)/shard_map/ppermute | solution.py:18
  194.9 3.7 %collective-permute-start.5 = (bf16[4,18,512]{2,1,0:T(8,128)(2,1)S(1)}, bf16[4,18,512]{2,1,0:T(8,128)(2,1)S(1)}, u32[]{:S(2)}, u32[]{:S(2)}) collective-permute-start(bf16[4,18,512]{2,1,0:T(8,128)(2,1)S(1)} %pad_maximum_fusion.2), channel_id=1, source_target_pairs={{0,1},{1,2},{2,3},{3,4},{4,5},{5,6},{6,7},{7,0},{8,9},{9,10},{10,1... | collective-permute-start | bytes 221192 | tf_op jit(solution)/shard_map/ppermute | solution.py:18
  198.6 9.5 %collective-permute-done.5 = bf16[4,18,512]{2,1,0:T(8,128)(2,1)S(1)} collective-permute-done((bf16[4,18,512]{2,1,0:T(8,128)(2,1)S(1)}, bf16[4,18,512]{2,1,0:T(8,128)(2,1)S(1)}, u32[]{:S(2)}, u32[]{:S(2)}) %collective-permute-start.5) | collective-permute-done | bytes 73760 | tf_op jit(solution)/shard_map/ppermute | solution.py:18
  208.7 1.4 copy.37
  (50 shorter events, 8.6 us)
Async XLA Ops:
  6.5 69.2 %copy-start = (bf16[512,1536]{1,0:T(8,128)(2,1)S(1)}, bf16[512,1536]{1,0:T(8,128)(2,1)}, u32[]{:S(2)}) copy-start(bf16[512,1536]{1,0:T(8,128)(2,1)} %param.9) | copy-start | bytes 4718596
  6.5 14.1 %copy-start.3 = (f32[16,72,72]{2,1,0:T(8,128)S(1)}, f32[16,72,72]{2,1,0:T(8,128)}, u32[]{:S(2)}) copy-start(f32[16,72,72]{2,1,0:T(8,128)} %param.13) | copy-start | bytes 995332
  6.5 151.3 %all-gather.3.cloned.1.call-start = ((), (), s32[]{:S(2)}) async-start(), calls=%async_computation | async-start | bytes 2359296 | tf_op jit(solution)/shard_map/all_gather | solution.py:81
  7.3 150.6 %all-gather.5.cloned.1.call-start = ((), (), s32[]{:S(2)}) async-start(), calls=%async_computation.1 | async-start | bytes 2359296 | tf_op jit(solution)/shard_map/all_gather | solution.py:84
  8.2 27.9 %collective-permute-start = (bf16[4,18,512]{2,0,1:T(4,128)(2,1)S(1)}, bf16[4,18,512]{2,0,1:T(4,128)(2,1)S(1)}, u32[]{:S(2)}, u32[]{:S(2)}) collective-permute-start(bf16[4,18,512]{2,0,1:T(4,128)(2,1)S(1)} %slice.46), channel_id=1, source_target_pairs={{0,7},{1,0},{2,1},{3,2},{4,3},{5,4},{6,5},{7,6},{8,15},{9,8},{10,9... | collective-permute-start | bytes 221192 | tf_op jit(solution)/shard_map/ppermute | solution.py:18
  16.8 5.5 %collective-permute-start.2 = (bf16[4,18]{0,1:T(8,128)(2,1)S(1)}, bf16[4,18]{0,1:T(8,128)(2,1)S(1)}, u32[]{:S(2)}, u32[]{:S(2)}) collective-permute-start(bf16[4,18]{0,1:T(8,128)(2,1)S(1)} %bitcast.37), channel_id=1, source_target_pairs={{0,7},{1,0},{2,1},{3,2},{4,3},{5,4},{6,5},{7,6},{8,15},{9,8},{10,9... | collective-permute-start | bytes 440 | tf_op jit(solution)/shard_map/ppermute | solution.py:18
  20.5 32.2 %copy-start.2 = (bf16[60,18,512]{2,0,1:T(8,128)(2,1)}, bf16[60,18,512]{2,0,1:T(8,128)(2,1)S(1)}, u32[]{:S(2)}) copy-start(bf16[60,18,512]{2,0,1:T(8,128)(2,1)S(1)} %slice.45) | copy-start | bytes 3317764
  22.3 13.4 %collective-permute-start.3 = (bf16[64,4]{0,1:T(4,128)(2,1)S(1)}, bf16[64,4]{0,1:T(4,128)(2,1)S(1)}, u32[]{:S(2)}, u32[]{:S(2)}) collective-permute-start(bf16[64,4]{0,1:T(4,128)(2,1)S(1)} %pad_maximum_fusion.4), channel_id=1, source_target_pairs={{0,504},{8,0},{16,8},{24,16},{32,24},{40,32},{48,40},{56,48},{64,5... | collective-permute-start | bytes 1544 | tf_op jit(solution)/shard_map/ppermute | solution.py:18
  36.2 31.4 %collective-permute-start.1 = (bf16[64,4,512]{2,0,1:T(8,128)(2,1)S(1)}, bf16[64,4,512]{2,0,1:T(8,128)(2,1)S(1)}, u32[]{:S(2)}, u32[]{:S(2)}) collective-permute-start(bf16[64,4,512]{2,0,1:T(8,128)(2,1)S(1)} %pad_maximum_fusion.1), channel_id=1, source_target_pairs={{0,504},{8,0},{16,8},{24,16},{32,24},{40,32},{48,40},{56,48},{64,5... | collective-permute-start | bytes 786440 | tf_op jit(solution)/shard_map/ppermute | solution.py:18
  115.4 2.6 %copy-start.4 = (f32[16,72,72]{1,2,0:T(8,128)S(1)}, f32[16,72,72]{1,2,0:T(8,128)}, u32[]{:S(2)}) copy-start(f32[16,72,72]{1,2,0:T(8,128)} %copy.33) | copy-start | bytes 995332
  115.4 2.6 %copy-start.6 = (pred[16,72,72]{1,2,0:T(8,128)(4,1)S(1)}, pred[16,72,72]{1,2,0:T(8,128)(4,1)}, u32[]{:S(2)}) copy-start(pred[16,72,72]{1,2,0:T(8,128)(4,1)} %broadcast_compare_fusion) | copy-start | bytes 248836
  151.8 2.8 %copy-start.5 = (bf16[512,512]{1,0:T(8,128)(2,1)S(1)}, bf16[512,512]{1,0:T(8,128)(2,1)}, u32[]{:S(2)}) copy-start(bf16[512,512]{1,0:T(8,128)(2,1)} %param.10) | copy-start | bytes 1572868
  168.9 25.9 %collective-permute-start.4 = (bf16[64,4,512]{2,1,0:T(4,128)(2,1)S(1)}, bf16[64,4,512]{2,1,0:T(4,128)(2,1)S(1)}, u32[]{:S(2)}, u32[]{:S(2)}) collective-permute-start(bf16[64,4,512]{2,1,0:T(4,128)(2,1)S(1)} %slice.69), channel_id=1, source_target_pairs={{0,8},{8,16},{16,24},{24,32},{32,40},{40,48},{48,56},{56,64},{64,7... | collective-permute-start | bytes 786440 | tf_op jit(solution)/shard_map/ppermute | solution.py:18
  194.8 15.3 %copy-start.1 = (bf16[512,1536]{1,0:T(8,128)(2,1)S(1)}, bf16[512,1536]{1,0:T(8,128)(2,1)}, u32[]{:S(2)}) copy-start(bf16[512,1536]{1,0:T(8,128)(2,1)} %param.9) | copy-start | bytes 4718596
  194.9 13.2 %collective-permute-start.5 = (bf16[4,18,512]{2,1,0:T(8,128)(2,1)S(1)}, bf16[4,18,512]{2,1,0:T(8,128)(2,1)S(1)}, u32[]{:S(2)}, u32[]{:S(2)}) collective-permute-start(bf16[4,18,512]{2,1,0:T(8,128)(2,1)S(1)} %pad_maximum_fusion.2), channel_id=1, source_target_pairs={{0,1},{1,2},{2,3},{3,4},{4,5},{5,6},{6,7},{7,0},{8,9},{9,10},{10,1... | collective-permute-start | bytes 221192 | tf_op jit(solution)/shard_map/ppermute | solution.py:18
Sparse Core Ops, SparseCore 0:
  9.4 79.7 all-gather.2
  91.3 65.2 all-gather.4
where the time goes:
time: 219 us; the launch traced here: 217 us
  local copies, waits for them, and re-layouts  71.3 us (33%)
  waiting for transfers between devices  48.4 us (22%)
  starting transfers between devices  44.1 us (20%)
  matrix products  34.1 us (16%)
  between operations  13.6 us (6%)
  other arithmetic  5.3 us (2%)
    ppermute x6, waiting for transfers between devices, from_behind(): return lax.ppermute(value, axis, pairs)  47.7 us
    ppermute x6, starting transfers between devices, from_behind(): return lax.ppermute(value, axis, pairs)  44.1 us
    convert_element_type x2, local copies, waits for them, and re-layouts, window_attention(): return outputs.reshape(count, WIN_TOK, D).astype(jnp.bfloat16)  13.7 us
    sub x1, matrix products, window_attention(): expo = jnp.exp(scores - largest)  10.3 us
    dot_general x1, matrix products, add_rows(): return jnp.dot(left, piece, preferred_element_type=jnp.float32)  8.69 us
    transpose x2, local copies, waits for them, and re-layouts, to_windows(): return shaped.transpose(0, 2, 1, 3, 4).reshape(-1, WIN_TOK, block.shape[2])  8.56 us
    reshape x1, local copies, waits for them, and re-layouts, to_windows(): return shaped.transpose(0, 2, 1, 3, 4).reshape(-1, WIN_TOK, block.shape[2])  8.36 us
    another operation x2, local copies, waits for them, and re-layouts, to_windows(): block.reshape(rows // WIN_ROWS, WIN_ROWS, cols // WIN_COLS, WIN_COLS, -1)  7.4 us
  transfers between devices with their start and end apart: 8, of which 5 were waited for; matrix products, arithmetic and copies ran while one was open for 45% of the time, Pallas kernels for 0%

commit v1 on v0

v1 whole, which is shorter than its diff:
```python
import jax
import jax.numpy as jnp
from jax import lax
from jax.experimental import pallas as pl
from jax.experimental.pallas import tpu as pltpu
from jax.sharding import PartitionSpec as P

MESH = pl.DeviceIdType.MESH
D = 512
HEADS = 16
ROWS = 64
COLS = 18
PITCH = 24
ID_LANES = 128
LOG2E = 1.4426950408889634
ORDER = (5, 6, 7, 8, 0, 1, 2, 3, 4)
MAIN = (5, 6, 7, 8, 0, 1, 2, 3, 4, 9, 10, 11, 12, 13)
HALO_ROWS = 256
MAIN_ROWS = 112
WIN_PITCH = 80
F32 = jnp.float32
BF16 = jnp.bfloat16


def norm(x):
    center = jnp.mean(x, axis=-1, keepdims=True)
    moved = x - center
    spread = jnp.mean(moved * moved, axis=-1, keepdims=True)
    return (moved * lax.rsqrt(spread + 1e-05)).astype(BF16)


def gelu(x):
    inner = 0.7978845608028654 * (x + 0.044715 * (x * x * x))
    return 0.5 * x * (1.0 + jnp.tanh(inner))


def kernel(
    field_h, marks_h, wqkv_h, wproj_h, wup_h, wdown_h, bias_h, out_h,
    field_v, marks_v, e, x_s, id_s, n_s, qw, idw, att, wq_v, wp_v, wu, wd,
    braw, btmp, bias_v, bias_in, out_t, acc,
    col_out, row_out, cor_out, col_in, row_in, cor_in, ret_col, ret_row, ret_cor, out_v,
    local_sem, halo_send, halo_recv, ret_send, ret_recv, w_send, w_recv, sib_send, sib_recv,
):
    lon = lax.axis_index("lon")
    lat = lax.axis_index("lat")
    core = lax.rem(lon, 2)
    west, east = lax.rem(lon + 63, 64), lax.rem(lon + 1, 64)
    north, south = lax.rem(lat + 7, 8), lax.rem(lat + 1, 8)
    sibling = lon + 1 - 2 * core
    far = lax.rem(lon + 32, 64)
    up_lon = jnp.where(lat == 7, far, lon)
    down_lon = jnp.where(lat == 0, far, lon)
    z_up = (up_lon, south)
    z_down = (down_lon, north)
    sib = (sibling, lat)

    def local(src, dst, i):
        return pltpu.make_async_copy(src, dst, local_sem.at[i])

    def remote(src, dst, ssem, rsem, dev):
        return pltpu.make_async_remote_copy(
            src_ref=src, dst_ref=dst, send_sem=ssem, recv_sem=rsem, device_id=dev, device_id_type=MESH
        )

    loads = [
        local(field_h, field_v, 0),
        local(marks_h, marks_v, 1),
        local(bias_h, bias_in, 2),
        local(wqkv_h, wq_v, 3),
        local(wproj_h, wp_v, 4),
        local(wup_h, wu.at[0], 5),
        local(wdown_h, wd.at[0], 6),
    ]
    for c in loads:
        c.start()

    partners = [(west, lat), (east, lat), (lon, north), (lon, south), (west, north), (east, south), z_up, z_down]
    barrier = pltpu.get_barrier_semaphore()
    for dev in partners:
        pl.semaphore_signal(barrier, inc=1, device_id=dev, device_id_type=MESH)
    pl.semaphore_wait(barrier, 8)

    def up(slot):
        return wu.at[slot, pl.ds(pl.multiple_of(core * 256, 256), 256), :]

    def down(slot):
        return wd.at[slot, pl.ds(pl.multiple_of(core * 128, 128), 128), :]

    def up_own():
        return wup_h.at[pl.ds(pl.multiple_of(core * 256, 256), 256), :]

    def down_own():
        return wdown_h.at[pl.ds(pl.multiple_of(core * 128, 128), 128), :]

    def chain(t):
        found = []
        for way in (0, 1):
            dev = (z_up, z_down)[way]
            for kind in (0, 1):
                if t == 3 and kind != way:
                    continue
                view = (up, down)[kind]
                if t == 0:
                    src = (up_own, down_own)[kind]()
                else:
                    src = view(t + 3 * way)
                dst = view(7 if t == 3 else t + 1 + 3 * way)
                i = t * 4 + way * 2 + kind
                found.append(remote(src, dst, w_send.at[i], w_recv.at[i], dev))
        return found

    def sib_copy(slot, kind):
        view = (up, down)[kind](slot)
        i = (slot - 1) * 2 + kind
        return remote(view, view, sib_send.at[i], sib_recv.at[i], sib)

    def progress(t):
        if t > 0:
            for c in chain(t - 1):
                c.wait_recv()
        if t < 4:
            for c in chain(t):
                c.start()
        if t > 0:
            for slot in (t, t + 3) if t < 4 else (7,):
                for kind in (0, 1):
                    sib_copy(slot, kind).start()

    progress(0)
    loads[0].wait()
    loads[1].wait()

    def spread_row(r, carry):
        x = field_v[r].astype(F32)
        m = marks_v[r].astype(F32)
        at = pl.ds(pl.multiple_of((r + 4) * PITCH, 8), COLS)
        for t in range(4):
            e[t, at, :] = x[:, 128 * t : 128 * (t + 1)]
        e[4, at, :] = m
        return carry

    lax.fori_loop(0, ROWS, spread_row, 0, unroll=4)

    def token(row, col):
        at = pl.ds(row * PITCH + col, 8, stride=PITCH)
        return jnp.concatenate([e[t, at, :] for t in range(5)], axis=-1)

    sub8 = lax.broadcasted_iota(jnp.int32, (8, D + ID_LANES), 0)

    def pack_cols(b, carry):
        parts = [token(8 + 8 * b, c) for c in range(4)]
        col_out[pl.ds(pl.multiple_of(b * 32, 32), 32), :] = jnp.concatenate(parts, axis=0).astype(BF16)
        return carry

    lax.fori_loop(0, 8, pack_cols, 0)
    send_col = remote(col_out, col_in, halo_send.at[0], halo_recv.at[0], (west, lat))
    send_col.start()
    cor_out[...] = jnp.concatenate([token(0, c) for c in range(4)], axis=0).astype(BF16)
    send_cor = remote(cor_out, cor_in, halo_send.at[1], halo_recv.at[1], (west, north))
    send_cor.start()
    pairs = []
    for g in range(7):
        pairs.append(jnp.where(sub8 < 4, token(4, 4 + 2 * g), token(0, 5 + 2 * g)))
    pairs.append(jnp.zeros_like(pairs[0]))
    row_out[...] = jnp.concatenate(pairs, axis=0).astype(BF16)
    send_row = remote(row_out, row_in, halo_send.at[2], halo_recv.at[2], (lon, north))
    send_row.start()

    loads[2].wait()

    def turn_bias(h, carry):
        braw[:, 0:72] = bias_in[h]
        first = [braw[pl.ds(c, 8, stride=9), :] for c in ORDER]
        first.append(jnp.zeros((56, 128), F32))
        btmp[...] = jnp.concatenate(first, axis=0).T
        second = [btmp[pl.ds(c, 8, stride=9), :] for c in ORDER]
        second.append(jnp.zeros((56, 128), F32))
        turned = jnp.concatenate(second, axis=0).T
        bias_v[pl.ds(pl.multiple_of(h * 72, 8), 72), :] = turned[0:72] * LOG2E
        return carry

    braw[...] = jnp.zeros_like(braw)
    lax.fori_loop(0, HEADS, turn_bias, 0)

    def keep(rows_at, block):
        x_s[rows_at, :] = block[:, 0:D]
        id_s[rows_at, :] = block[:, D:]

    def main_at(m):
        return pl.multiple_of(HALO_ROWS + MAIN_ROWS * m, 16)

    def gather_band(b, carry):
        start = HALO_ROWS + MAIN_ROWS * (b + 1)
        for i in range(7):
            pair = [token(8 + 8 * b, 4 + MAIN[2 * i + j]) for j in (0, 1)]
            keep(pl.ds(pl.multiple_of(start + 16 * i, 16), 16), jnp.concatenate(pair, axis=0).astype(BF16))
        return carry

    lax.fori_loop(0, 7, gather_band, 0)

    loads[3].wait()

    def qkv_rows(at, size):
        x = x_s[pl.ds(at, size), :].astype(F32)
        return norm(x)

    def qkv_main(m, carry):
        at = main_at(m)
        b = lax.rem(m + 7, 8)
        normed = qkv_rows(at, MAIN_ROWS)
        base = pl.multiple_of(b * 2 * WIN_PITCH, 16)
        other = pl.multiple_of(b * 2 * WIN_PITCH + WIN_PITCH + 32, 16)
        fill = jnp.zeros((8, D), F32)
        for part in range(3):
            lanes = slice(part * D, (part + 1) * D)
            res = jnp.dot(normed, wq_v[:, lanes], preferred_element_type=F32)
            qw[pl.ds(base, 80), lanes] = jnp.concatenate([res[0:72], fill], axis=0).astype(BF16)
            qw[pl.ds(other, 48), lanes] = jnp.concatenate([res[72:112], fill], axis=0).astype(BF16)
        ids = id_s[pl.ds(at, MAIN_ROWS), :].astype(F32)
        fill = jnp.zeros((8, ID_LANES), F32)
        idw[pl.ds(base, 80), :] = jnp.concatenate([ids[0:72], fill], axis=0).astype(BF16)
        idw[pl.ds(other, 48), :] = jnp.concatenate([ids[72:112], fill], axis=0).astype(BF16)
        return carry

    lax.fori_loop(1, 8, qkv_main, 0)

    send_row.wait_recv()
    halo = row_in[...].astype(F32)
    ready = []
    for c in range(14):
        piece = halo[8 * (c // 2) : 8 * (c // 2) + 8]
        if c % 2 == 0:
            piece = jnp.concatenate([piece[4:8], piece[0:4]], axis=0)
        ready.append(jnp.where(sub8 < 4, token(64, 4 + c), piece))
    for i in range(7):
        pair = [ready[MAIN[2 * i + j]] for j in (0, 1)]
        keep(pl.ds(HALO_ROWS + 16 * i, 16), jnp.concatenate(pair, axis=0).astype(BF16))
    qkv_main(0, 0)

    send_col.wait_recv()
    send_cor.wait_recv()
    keep(pl.ds(0, 224), col_in[0:224, :])
    mine = col_in[224:256, :].astype(F32)
    corner = cor_in[...].astype(F32)
    sub32 = lax.rem(lax.broadcasted_iota(jnp.int32, (32, D + ID_LANES), 0), 8)
    keep(pl.ds(224, 32), jnp.where(sub32 < 4, mine, corner).astype(BF16))

    def qkv_halo(b, carry):
        at = pl.multiple_of(b * 64, 64)
        normed = qkv_rows(at, 64)
        for part in range(3):
            lanes = slice(part * D, (part + 1) * D)
            res = jnp.dot(normed, wq_v[:, lanes], preferred_element_type=F32).astype(BF16)
            for i in (0, 1):
                dst = pl.multiple_of((4 * b + 2 * i + 1) * WIN_PITCH, 16)
                qw[pl.ds(dst, 32), lanes] = res[32 * i : 32 * i + 32]
        for i in (0, 1):
            dst = pl.multiple_of((4 * b + 2 * i + 1) * WIN_PITCH, 16)
            idw[pl.ds(dst, 32), :] = id_s[pl.ds(pl.multiple_of(b * 64 + 32 * i, 32), 32), :]
        return carry

    lax.fori_loop(0, 4, qkv_halo, 0)

    lane256 = lax.broadcasted_iota(jnp.int32, (80, 256), 1)
    block_of = lax.rem(lane256, 128) // 32
    low = lane256 < 128
    zero80 = jnp.zeros((80, 256), BF16)
    zero48 = jnp.zeros((48, 256), BF16)
    block72 = block_of[0:72]
    scale = LOG2E * 32 ** (-0.5)

    def blocks(v):
        return jnp.concatenate([jnp.where(low, v, zero80), zero48, jnp.where(low, zero80, v), zero48], axis=0)

    def window(w):
        at = pl.ds(pl.multiple_of(w * WIN_PITCH, 16), WIN_PITCH)
        ids = idw[at, :]
        wide = jnp.concatenate([ids, jnp.zeros((48, ID_LANES), BF16)], axis=0)
        same = lax.dot_general(ids, wide, (((1,), (1,)), ((), ())), preferred_element_type=F32)
        shut = (same[0:72] - 1.0) * 1e30
        halves = []
        for g in range(2):
            lanes = slice(256 * g, 256 * (g + 1))
            qg = qw[at, 256 * g : 256 * g + 256]
            kg = qw[at, D + 256 * g : D + 256 * g + 256]
            vg = qw[at, 2 * D + 256 * g : 2 * D + 256 * g + 256]
            qb = jnp.concatenate([jnp.where(block_of == j, qg, zero80) for j in range(4)], axis=0)
            scores = lax.dot_general(qb, blocks(kg), (((1,), (1,)), ((), ())), preferred_element_type=F32)
            rows = []
            for j in range(4):
                sides = []
                for t in range(2):
                    head = 8 * g + 4 * t + j
                    s = scores[80 * j : 80 * j + 72, 128 * t : 128 * t + 128] * scale
                    s = s + bias_v[72 * head : 72 * head + 72, :] + shut
                    ex = jnp.exp2(s - jnp.max(s, axis=-1, keepdims=True))
                    sides.append(ex * (1.0 / jnp.sum(ex, axis=-1, keepdims=True)))
                rows.append(jnp.concatenate(sides, axis=-1))
                rows.append(jnp.zeros((8, 256), F32))
            probs = jnp.concatenate(rows, axis=0).astype(BF16)
            res = jnp.dot(probs, blocks(vg), preferred_element_type=F32)
            o = res[0:72]
            for j in range(1, 4):
                o = jnp.where(block72 == j, res[80 * j : 80 * j + 72], o)
            halves.append(o)
        return jnp.concatenate(halves, axis=-1)

    def attend_band(b, carry):
        first = window(2 * b)
        second = window(2 * b + 1)
        m = lax.rem(b + 1, 8)
        att[pl.ds(pl.multiple_of(b * 32, 32), 32), :] = second[0:32].astype(BF16)
        att[pl.ds(main_at(m), MAIN_ROWS), :] = jnp.concatenate([first, second[32:72]], axis=0).astype(BF16)
        for t in range(1, 5):
            @pl.when(b == 2 * t - 2)
            def _():
                progress(t)
        return carry

    lax.fori_loop(0, 8, attend_band, 0)

    for slot in range(1, 8):
        for kind in (0, 1):
            sib_copy(slot, kind).wait_recv()
    loads[4].wait()
    loads[5].wait()
    loads[6].wait()

    def mlp(start, size):
        at = pl.ds(start, size)
        mixed = x_s[at, :].astype(F32) + jnp.dot(att[at, :], wp_v[...], preferred_element_type=F32)
        mixed = mixed.astype(BF16).astype(F32)
        acc[0:size, :] = mixed
        n_s[0:size, :] = norm(mixed)

        def hidden(s, carry):
            h = gelu(jnp.dot(n_s[0:size, :], wu[s], preferred_element_type=F32)).astype(BF16)
            acc[0:size, :] += jnp.dot(h, wd[s], preferred_element_type=F32)
            return carry

        lax.fori_loop(0, 8, hidden, 0)
        out_t[at, :] = acc[0:size, :].astype(BF16)

    mlp(0, 368)
    backs = [
        remote(out_t.at[pl.ds(0, 256), :], ret_col, ret_send.at[0], ret_recv.at[0], (east, lat)),
        remote(out_t.at[pl.ds(224, 32), :], ret_cor, ret_send.at[1], ret_recv.at[1], (east, south)),
        remote(out_t.at[pl.ds(256, 112), :], ret_row, ret_send.at[2], ret_recv.at[2], (lon, south)),
    ]
    for c in backs:
        c.start()
    mlp(368, 400)
    mlp(768, 384)

    def put(row, col, block):
        at = pl.ds(row * PITCH + col, 8, stride=PITCH)
        for t in range(4):
            e[t, at, :] = block[:, 128 * t : 128 * (t + 1)]

    backs[1].wait_recv()
    backs[2].wait_recv()
    north_rows = ret_row[...].astype(F32)
    for i in range(14):
        put(0, 4 + MAIN[i], north_rows[8 * i : 8 * i + 8])
    north_cor = ret_cor[...].astype(F32)
    for i in range(4):
        put(0, i, north_cor[8 * i : 8 * i + 8])

    def put_main(b, carry):
        block = out_t[pl.ds(main_at(lax.rem(b + 1, 8)), MAIN_ROWS), :].astype(F32)
        for i in range(14):
            put(8 + 8 * b, 4 + MAIN[i], block[8 * i : 8 * i + 8])
        return carry

    lax.fori_loop(0, 8, put_main, 0)
    backs[0].wait_recv()

    def put_halo(b, carry):
        block = ret_col[pl.ds(pl.multiple_of(b * 32, 32), 32), :].astype(F32)
        for i in range(4):
            put(8 + 8 * b, i, block[8 * i : 8 * i + 8])
        return carry

    lax.fori_loop(0, 8, put_halo, 0)

    def finish_row(r, carry):
        at = pl.ds(pl.multiple_of((r + 4) * PITCH, 8), COLS)
        out_v[r] = jnp.concatenate([e[t, at, :] for t in range(4)], axis=-1).astype(BF16)
        return carry

    lax.fori_loop(0, ROWS, finish_row, 0, unroll=4)
    store = local(out_v, out_h, 7)
    store.start()
    store.wait()

    for t in range(4):
        for c in chain(t):
            c.wait_send()
    for slot in range(1, 8):
        for kind in (0, 1):
            sib_copy(slot, kind).wait_send()
    for c in (send_col, send_cor, send_row, *backs):
        c.wait_send()


def block(field, region, w_qkv, w_proj, w_up, w_down, position_bias):
    lanes = lax.broadcasted_iota(jnp.int32, (ROWS, COLS, ID_LANES), 2)
    marks = (region[:, :, None] == lanes).astype(BF16)
    wide = D + ID_LANES
    vm = pltpu.VMEM
    scratch = [
        vm((ROWS, COLS, D), BF16),
        vm((ROWS, COLS, ID_LANES), BF16),
        vm((5, 72 * PITCH, 128), F32),
        vm((1152, D), BF16),
        vm((1152, ID_LANES), BF16),
        vm((400, D), BF16),
        vm((16 * WIN_PITCH, 3 * D), BF16),
        vm((16 * WIN_PITCH, ID_LANES), BF16),
        vm((1152, D), BF16),
        vm((D, 3 * D), BF16),
        vm((D, D), BF16),
        vm((8, D, 256), BF16),
        vm((8, 256, D), BF16),
        vm((72, 128), F32),
        vm((128, 128), F32),
        vm((HEADS * 72, 128), F32),
        vm((HEADS, 72, 72), F32),
        vm((1152, D), BF16),
        vm((400, D), F32),
        vm((256, wide), BF16),
        vm((64, wide), BF16),
        vm((32, wide), BF16),
        vm((256, wide), BF16),
        vm((64, wide), BF16),
        vm((32, wide), BF16),
        vm((256, D), BF16),
        vm((112, D), BF16),
        vm((32, D), BF16),
        vm((ROWS, COLS, D), BF16),
        pltpu.SemaphoreType.DMA((8,)),
        pltpu.SemaphoreType.DMA((3,)),
        pltpu.SemaphoreType.DMA((3,)),
        pltpu.SemaphoreType.DMA((3,)),
        pltpu.SemaphoreType.DMA((3,)),
        pltpu.SemaphoreType.DMA((16,)),
        pltpu.SemaphoreType.DMA((16,)),
        pltpu.SemaphoreType.DMA((14,)),
        pltpu.SemaphoreType.DMA((14,)),
    ]
    return pl.pallas_call(
        kernel,
        out_shape=jax.ShapeDtypeStruct((ROWS, COLS, D), BF16),
        in_specs=[pl.BlockSpec(memory_space=pl.ANY)] * 7,
        out_specs=pl.BlockSpec(memory_space=pl.ANY),
        scratch_shapes=scratch,
        compiler_params=pltpu.CompilerParams(
            collective_id=0, has_side_effects=True, vmem_limit_bytes=58 * 1024 * 1024
        ),
    )(field, marks, w_qkv, w_proj, w_up, w_down, position_bias)


def solution(mesh):
    placed = (P("lat", "lon", None), P("lat", "lon"), P(), P(), P(None, "lat"), P("lat", None), P())
    return jax.shard_map(
        block, mesh=mesh, in_specs=placed, out_specs=P("lat", "lon", None), check_vma=False
    )
```

time: 219 us -> 103 us (0.47)
  the two profiles are of different devices: /device:TPU:0 before, /device:TPU:31 now
where the time goes in v1:
time: 103 us
  Pallas kernels  95.4 us (93%)
  local copies, waits for them, and re-layouts  6.66 us (6%)
    pallas_call x1, Pallas kernels, block(): pl.pallas_call(kernel, out_shape=jax.ShapeDtypeStruct((ROWS, COLS, D), BF...  95.4 us
    unnamed x2, local copies, waits for them, and re-layouts  3.88 us
    pallas_call x1, local copies, waits for them, and re-layouts, block(): pl.pallas_call(kernel, out_shape=jax.ShapeDtypeStruct((ROWS, COLS, D), BF...  2.78 us

profile of v1, /device:TPU:31, one launch (start us, length us, event | category | flops | bytes accessed | tf_op | source)
XLA Modules:
  0.0 103.0 jit_solution(4761415340844103102)
XLA Ops:
  0.0 0.8 copy.8
  0.8 1.0 fusion.marks_h
  1.8 3.1 %copy.9.field_h = bf16[64,18,512]{2,1,0:T(8,128)(2,1)} copy(bf16[64,18,512]{2,0,1:T(8,128)(2,1)} %param.7) | data formatting | bytes 2359296 | tf_op args[0]
  4.9 95.4 %shard_map.73 = bf16[64,18,512]{2,1,0:T(8,128)(2,1)} custom-call(bf16[64,18,512]{2,1,0:T(8,128)(2,1)} %copy.9.field_h, bf16[64,18,128]{2,1,0:T(8,128)(2,1)} %fusion.marks_h, bf16[512,1536]{1,0:T(8,128)(2,1)} %wqkv_h.1, bf16[512,512]{1,0:T(8,128)(2,1)} %wproj_h.1, bf16[512,256]{1,0:T(8,128)(2,1)} %wup_h.1, bf16[256,512]{1,0:T(8,128)(2,1)} %wdown_h.1, ...), custom_call_target="tpu_custom_call" | custom-call | tf_op jit(solution)/shard_map/pallas_call | solution.py:451
  100.3 2.8 %copy.10 = bf16[64,18,512]{2,0,1:T(8,128)(2,1)} copy(bf16[64,18,512]{2,1,0:T(8,128)(2,1)} %shard_map.73) | data formatting | bytes 2359296 | tf_op jit(solution)/shard_map/pallas_call | solution.py:451

commit v2 on v1

v2 whole, which is shorter than its diff:
```python
import jax
import jax.numpy as jnp
from jax import lax
from jax.experimental import pallas as pl
from jax.experimental.pallas import tpu as pltpu
from jax.sharding import PartitionSpec as P

MESH = pl.DeviceIdType.MESH
D = 512
HEADS = 16
ROWS = 64
COLS = 18
LOG2E = 1.4426950408889634
ORDER = (5, 6, 7, 8, 0, 1, 2, 3, 4)
PAIRS = ((5, 6), (7, 8), (0, 1), (2, 3), (4, 13), (9, 10), (11, 12))
LAST = (5, 6, 7, 8, 0, 1, 2, 3, 4, 9, 10, 11, 12, 13)
LAST_AT = 256
PAIR_AT = 368
PAIR_ROWS = 112
WIN_PITCH = 80
F32 = jnp.float32
BF16 = jnp.bfloat16
NT = (((1,), (1,)), ((), ()))


def norm(x):
    center = jnp.mean(x, axis=-1, keepdims=True)
    moved = x - center
    spread = jnp.mean(moved * moved, axis=-1, keepdims=True)
    return (moved * lax.rsqrt(spread + 1e-05)).astype(BF16)


def gelu(x):
    inner = 0.7978845608028654 * (x + 0.044715 * (x * x * x))
    return 0.5 * x * (1.0 + jnp.tanh(inner))


def swap4(x):
    return jnp.concatenate([x[4:8], x[0:4]], axis=0)


def kernel(
    field_h, region_h, wqkv_h, wproj_h, wup_h, wdown_h, bias_h, out_h,
    field_v, region_v, x_s, n_s, qw, idw, att, wq_v, wp_v, wu, wd,
    braw, btmp, bias_v, bias_in, out_t, acc, hot,
    reg_out, reg_e, reg_s, reg_se, row_out, col_in, row_in, cor_in,
    back_row, back_cor, ret_col, ret_row, ret_cor, out_v,
    local_sem, out_sem, halo_send, halo_recv, ret_send, ret_recv, w_send, w_recv, sib_send, sib_recv,
):
    lon = lax.axis_index("lon")
    lat = lax.axis_index("lat")
    core = lax.rem(lon, 2)
    west, east = lax.rem(lon + 63, 64), lax.rem(lon + 1, 64)
    north, south = lax.rem(lat + 7, 8), lax.rem(lat + 1, 8)
    sibling = lon + 1 - 2 * core
    far = lax.rem(lon + 32, 64)
    z_up = (jnp.where(lat == 7, far, lon), south)
    z_down = (jnp.where(lat == 0, far, lon), north)
    sib = (sibling, lat)

    def local(src, dst, i):
        return pltpu.make_async_copy(src, dst, local_sem.at[i])

    def remote(src, dst, ssem, rsem, dev):
        return pltpu.make_async_remote_copy(
            src_ref=src, dst_ref=dst, send_sem=ssem, recv_sem=rsem, device_id=dev, device_id_type=MESH
        )

    loads = [
        local(field_h, field_v, 0),
        local(region_h, region_v, 1),
        local(bias_h, bias_in, 2),
        local(wqkv_h, wq_v, 3),
        local(wproj_h, wp_v, 4),
        local(wup_h, wu.at[0], 5),
        local(wdown_h, wd.at[0], 6),
    ]
    for c in loads:
        c.start()

    partners = [(west, lat), (east, lat), (lon, north), (lon, south), (west, north), (east, south), z_up, z_down]
    barrier = pltpu.get_barrier_semaphore()
    for dev in partners:
        pl.semaphore_signal(barrier, inc=1, device_id=dev, device_id_type=MESH)
    pl.semaphore_wait(barrier, 8)

    def up(slot):
        return wu.at[slot, pl.ds(pl.multiple_of(core * 256, 256), 256), :]

    def down(slot):
        return wd.at[slot, pl.ds(pl.multiple_of(core * 128, 128), 128), :]

    def up_own():
        return wup_h.at[pl.ds(pl.multiple_of(core * 256, 256), 256), :]

    def down_own():
        return wdown_h.at[pl.ds(pl.multiple_of(core * 128, 128), 128), :]

    def chain(t):
        found = []
        for way in (0, 1):
            dev = (z_up, z_down)[way]
            for kind in (0, 1):
                if t == 3 and kind != way:
                    continue
                view = (up, down)[kind]
                if t == 0:
                    src = (up_own, down_own)[kind]()
                else:
                    src = view(t + 3 * way)
                dst = view(7 if t == 3 else t + 1 + 3 * way)
                i = t * 4 + way * 2 + kind
                found.append(remote(src, dst, w_send.at[i], w_recv.at[i], dev))
        return found

    def sib_copy(slot, kind):
        view = (up, down)[kind](slot)
        i = (slot - 1) * 2 + kind
        return remote(view, view, sib_send.at[i], sib_recv.at[i], sib)

    def progress(t):
        if t > 0:
            for c in chain(t - 1):
                c.wait_recv()
        if t < 4:
            for c in chain(t):
                c.start()
        if t > 0:
            for slot in (t, t + 3) if t < 4 else (7,):
                for kind in (0, 1):
                    sib_copy(slot, kind).start()

    send_col = remote(field_h.at[pl.ds(0, 4)], col_in, halo_send.at[0], halo_recv.at[0], (west, lat))
    send_row = remote(row_out.at[pl.ds(16, 64), :], row_in, halo_send.at[1], halo_recv.at[1], (lon, north))
    send_cor = remote(row_out.at[pl.ds(0, 16), :], cor_in, halo_send.at[2], halo_recv.at[2], (west, north))
    send_ids = [
        remote(reg_out, reg_e, halo_send.at[3], halo_recv.at[3], (west, lat)),
        remote(reg_out, reg_s, halo_send.at[4], halo_recv.at[4], (lon, north)),
        remote(reg_out, reg_se, halo_send.at[5], halo_recv.at[5], (west, north)),
    ]
    sub8 = lax.broadcasted_iota(jnp.int32, (8, D), 0)

    def send_halos():
        send_col.start()
        loads[1].wait()
        reg_out[...] = jnp.zeros_like(reg_out)
        reg_out[0:18, 0:64] = region_v[...]
        for c in send_ids:
            c.start()
        loads[0].wait()
        tops = [field_v[c, 0:16, :].astype(F32)[0:8] for c in range(COLS)]
        packed = [jnp.where(sub8 < 4, tops[2 * i], swap4(tops[2 * i + 1])) for i in range(9)]
        packed.append(jnp.zeros_like(packed[0]))
        row_out[...] = jnp.concatenate(packed, axis=0).astype(BF16)
        send_row.start()
        send_cor.start()

    def turn_biases():
        loads[2].wait()
        braw[...] = jnp.zeros_like(braw)

        def turn_bias(h, carry):
            braw[:, 0:72] = bias_in[h]
            first = [braw[pl.ds(c, 8, stride=9), :] for c in ORDER]
            first.append(jnp.zeros((56, 128), F32))
            btmp[...] = jnp.concatenate(first, axis=0).T
            second = [btmp[pl.ds(c, 8, stride=9), :] for c in ORDER]
            second.append(jnp.zeros((56, 128), F32))
            turned = jnp.concatenate(second, axis=0).T
            bias_v[pl.ds(pl.multiple_of(h * 72, 8), 72), :] = turned[0:72] * LOG2E
            return carry

        lax.fori_loop(0, HEADS, turn_bias, 0)

    lane24 = lax.broadcasted_iota(jnp.int32, (24, 128), 1)
    lane64 = lax.broadcasted_iota(jnp.int32, (64, 128), 1)

    def id_rows(here, below):
        moved = jnp.where(lane24 < 60, pltpu.roll(here, 124, 1), pltpu.roll(below, 60, 1))
        tall = jnp.concatenate([moved, jnp.zeros((104, 128), F32)], axis=0)
        return tall.T[0:64]

    def hot_col(table, c):
        wide = jnp.broadcast_to(table[:, c : c + 1], (64, 128))
        return (wide == lane64.astype(F32)).astype(F32)

    def put_ids(s, pos, top, low, bands):
        for b in bands:
            rows = [top[8 * b : 8 * b + 8], low[8 * b : 8 * b + 8]]
            idw[pl.ds((2 * b + s) * WIN_PITCH + 16 * pos, 16), :] = jnp.concatenate(rows, axis=0).astype(BF16)

    def main_ids(below, bands):
        table = id_rows(reg_out[...].astype(F32), below)
        zero = jnp.zeros((64, 128), F32)
        for i, (a, z) in enumerate(PAIRS):
            first, second = hot_col(table, a + 4), hot_col(table, z + 4)
            if i < 4:
                put_ids(0, i, first, second, bands)
            elif i == 4:
                put_ids(0, 4, first, zero, bands)
                put_ids(1, 4, second, zero, bands)
            else:
                put_ids(1, i - 3, first, second, bands)

    def halo_ids():
        table = id_rows(reg_e[...].astype(F32), reg_se[...].astype(F32))
        for i in (0, 1):
            put_ids(1, i, hot_col(table, 2 * i), hot_col(table, 2 * i + 1), range(8))

    def gather_main():
        for i, pair in enumerate(PAIRS):
            rows = [field_v[c + 4].astype(F32)[4:60] for c in pair]
            block = jnp.concatenate(rows, axis=0)
            at = pl.ds(PAIR_AT + PAIR_ROWS * i, PAIR_ROWS)
            x_s[at, :] = block.astype(BF16)
            n_s[at, :] = norm(block)

    def scatter(part, i, res):
        lanes = part
        for b in range(7):
            first, second = res[8 * b : 8 * b + 8], res[56 + 8 * b : 64 + 8 * b]
            if i == 4:
                fill = jnp.zeros_like(first)
                for s, piece in ((0, first), (1, second)):
                    both = jnp.concatenate([piece, fill], axis=0).astype(BF16)
                    qw[pl.ds((2 * b + s) * WIN_PITCH + 64, 16), lanes] = both
            else:
                s, pos = (0, i) if i < 4 else (1, i - 3)
                both = jnp.concatenate([first, second], axis=0).astype(BF16)
                qw[pl.ds((2 * b + s) * WIN_PITCH + 16 * pos, 16), lanes] = both

    def qkv_main():
        loads[3].wait()

        def step(n, carry):
            lanes = pl.ds(pl.multiple_of(n * 256, 256), 256)
            res = jnp.dot(n_s[pl.ds(PAIR_AT, 784), :], wq_v[:, lanes], preferred_element_type=F32)
            for i in range(7):
                scatter(lanes, i, res[PAIR_ROWS * i : PAIR_ROWS * (i + 1)])
            return carry

        lax.fori_loop(0, 6, step, 0)

    def gather_halo():
        send_row.wait_recv()
        below = row_in[...].astype(F32)
        ready = {}
        for c in range(14):
            piece = below[8 * (c // 2) : 8 * (c // 2) + 8]
            if c % 2 == 0:
                piece = swap4(piece)
            mine = swap4(field_v[c + 4, 48:64, :].astype(F32)[8:16])
            ready[c] = jnp.where(sub8 < 4, mine, piece)
        block = jnp.concatenate([ready[c] for c in LAST], axis=0)
        at = pl.ds(LAST_AT, PAIR_ROWS)
        x_s[at, :] = block.astype(BF16)
        n_s[at, :] = norm(block)
        send_cor.wait_recv()
        corner = cor_in[...].astype(F32)
        send_col.wait_recv()
        for c in range(4):
            piece = corner[8 * (c // 2) : 8 * (c // 2) + 8]
            piece = piece[0:4] if c % 2 == 0 else piece[4:8]
            block = jnp.concatenate([col_in[c].astype(F32)[4:64], piece], axis=0)
            at = pl.ds(64 * c, 64)
            x_s[at, :] = block.astype(BF16)
            n_s[at, :] = norm(block)

    def qkv_halo():
        def step(n, carry):
            lanes = pl.ds(pl.multiple_of(n * 256, 256), 256)
            res = jnp.dot(n_s[pl.ds(0, PAIR_AT), :], wq_v[:, lanes], preferred_element_type=F32)
            for i in range(2):
                for b in range(8):
                    both = [res[64 * (2 * i + j) + 8 * b : 64 * (2 * i + j) + 8 * b + 8] for j in (0, 1)]
                    at = pl.ds((2 * b + 1) * WIN_PITCH + 16 * i, 16)
                    qw[at, lanes] = jnp.concatenate(both, axis=0).astype(BF16)
            last = res[LAST_AT:PAIR_AT]
            fill = jnp.zeros((8, 256), F32)
            qw[pl.ds(14 * WIN_PITCH, 80), lanes] = jnp.concatenate([last[0:72], fill], axis=0).astype(BF16)
            tail = [last[72:104], last[104:112], fill]
            qw[pl.ds(15 * WIN_PITCH + 32, 48), lanes] = jnp.concatenate(tail, axis=0).astype(BF16)
            return carry

        lax.fori_loop(0, 6, step, 0)

    lane256 = lax.broadcasted_iota(jnp.int32, (80, 256), 1)
    block_of = lax.rem(lane256, 128) // 32
    low = lane256 < 128
    zero80 = jnp.zeros((80, 256), BF16)
    zero48 = jnp.zeros((48, 256), BF16)
    block72 = block_of[0:72]
    scale = LOG2E * 32 ** (-0.5)

    def blocks(v):
        return jnp.concatenate([jnp.where(low, v, zero80), zero48, jnp.where(low, zero80, v), zero48], axis=0)

    def window(w):
        at = pl.ds(pl.multiple_of(w * WIN_PITCH, 16), WIN_PITCH)
        ids = idw[at, :]
        wide = jnp.concatenate([ids, jnp.zeros((48, 128), BF16)], axis=0)
        same = lax.dot_general(ids, wide, NT, preferred_element_type=F32)
        shut = (same[0:72] - 1.0) * 1e30
        halves = []
        for g in range(2):
            qg = qw[at, 256 * g : 256 * g + 256]
            kg = qw[at, D + 256 * g : D + 256 * g + 256]
            vg = qw[at, 2 * D + 256 * g : 2 * D + 256 * g + 256]
            qb = jnp.concatenate([jnp.where(block_of == j, qg, zero80) for j in range(4)], axis=0)
            scores = lax.dot_general(qb, blocks(kg), NT, preferred_element_type=F32)
            rows = []
            for j in range(4):
                sides = []
                for t in range(2):
                    head = 8 * g + 4 * t + j
                    s = scores[80 * j : 80 * j + 72, 128 * t : 128 * t + 128] * scale
                    s = s + bias_v[72 * head : 72 * head + 72, :] + shut
                    ex = jnp.exp2(s - jnp.max(s, axis=-1, keepdims=True))
                    sides.append(ex * (1.0 / jnp.sum(ex, axis=-1, keepdims=True)))
                rows.append(jnp.concatenate(sides, axis=-1))
                rows.append(jnp.zeros((8, 256), F32))
            probs = jnp.concatenate(rows, axis=0).astype(BF16)
            res = jnp.dot(probs, blocks(vg), preferred_element_type=F32)
            o = res[0:72]
            for j in range(1, 4):
                o = jnp.where(block72 == j, res[80 * j : 80 * j + 72], o)
            halves.append(o)
        return jnp.concatenate(halves, axis=-1)

    def attend_band(b, carry):
        att[pl.ds(pl.multiple_of(2 * b * WIN_PITCH, 16), 72), :] = window(2 * b)
        att[pl.ds(pl.multiple_of(2 * b * WIN_PITCH + WIN_PITCH, 16), 72), :] = window(2 * b + 1)
        for t in range(1, 5):
            @pl.when(b == 2 * t - 2)
            def _():
                progress(t)
        return carry

    def attention():
        lax.fori_loop(0, 8, attend_band, 0)

    def attended(w, pos):
        return att[w * WIN_PITCH + 8 * pos : w * WIN_PITCH + 8 * pos + 8, :]

    def order_attended():
        for c in range(4):
            block = [attended(2 * b + 1, c) for b in range(8)]
            n_s[64 * c : 64 * c + 64, :] = jnp.concatenate(block, axis=0).astype(BF16)
        block = [att[14 * WIN_PITCH : 14 * WIN_PITCH + 72, :], att[15 * WIN_PITCH + 32 : 15 * WIN_PITCH + 72, :]]
        n_s[LAST_AT:PAIR_AT, :] = jnp.concatenate(block, axis=0).astype(BF16)
        for i, pair in enumerate(PAIRS):
            block = []
            for j in (0, 1):
                s, pos = (0, 2 * i + j) if i < 4 else (1, 2 * (i - 3) + j)
                if i == 4:
                    s, pos = j, 8
                block += [attended(2 * b + s, pos) for b in range(7)]
            n_s[PAIR_AT + 112 * i : PAIR_AT + 112 * i + 112, :] = jnp.concatenate(block, axis=0).astype(BF16)

    def await_weights():
        for slot in range(1, 8):
            for kind in (0, 1):
                sib_copy(slot, kind).wait_recv()
        for c in loads[4:7]:
            c.wait()

    def mlp(start, size):
        at = pl.ds(start, size)
        mixed = x_s[at, :].astype(F32) + jnp.dot(n_s[at, :], wp_v[...], preferred_element_type=F32)
        mixed = mixed.astype(BF16).astype(F32)
        acc[0:size, :] = mixed
        n_s[at, :] = norm(mixed)

        def hidden(s, carry):
            h = gelu(jnp.dot(n_s[at, :], wu[s], preferred_element_type=F32)).astype(BF16)
            acc[0:size, :] += jnp.dot(h, wd[s], preferred_element_type=F32)
            return carry

        lax.fori_loop(0, 8, hidden, 0)
        out_t[at, :] = acc[0:size, :].astype(BF16)

    backs = [
        remote(out_t.at[pl.ds(0, 256), :], ret_col, ret_send.at[0], ret_recv.at[0], (east, lat)),
        remote(back_cor, ret_cor, ret_send.at[1], ret_recv.at[1], (east, south)),
        remote(back_row, ret_row, ret_send.at[2], ret_recv.at[2], (lon, south)),
    ]

    def send_back():
        backs[0].start()
        ends = [out_t[64 * c + 48 : 64 * c + 64, :].astype(F32)[8:16] for c in range(4)]
        packed = [jnp.where(sub8 < 4, swap4(ends[2 * i]), ends[2 * i + 1]) for i in range(2)]
        back_cor[...] = jnp.concatenate(packed, axis=0).astype(BF16)
        backs[1].start()
        last = out_t[LAST_AT:PAIR_AT, :].astype(F32)
        packed = []
        for i in range(7):
            packed.append(jnp.where(sub8 < 4, swap4(last[16 * i : 16 * i + 8]), last[16 * i + 8 : 16 * i + 16]))
        packed.append(jnp.zeros_like(packed[0]))
        back_row[...] = jnp.concatenate(packed, axis=0).astype(BF16)
        backs[2].start()

    stores = []

    def store_col(c):
        found = pltpu.make_async_copy(out_v.at[c], out_h.at[c], out_sem.at[c])
        found.start()
        stores.append(found)

    def head4(packed, i):
        piece = packed[8 * (i // 2) : 8 * (i // 2) + 8]
        return piece[0:4] if i % 2 == 0 else piece[4:8]

    def finish_main():
        backs[2].wait_recv()
        above = ret_row[...].astype(F32)
        last = out_t[LAST_AT:PAIR_AT, :].astype(F32)
        for i, pair in enumerate(PAIRS):
            block = out_t[PAIR_AT + 112 * i : PAIR_AT + 112 * i + 112, :].astype(F32)
            for j, c in enumerate(pair):
                k = LAST.index(c)
                parts = [head4(above, k), block[56 * j : 56 * j + 56], last[8 * k : 8 * k + 4]]
                out_v[c + 4] = jnp.concatenate(parts, axis=0).astype(BF16)
                store_col(c + 4)

    def finish_halo():
        backs[1].wait_recv()
        above = ret_cor[...].astype(F32)
        backs[0].wait_recv()
        for c in range(4):
            block = ret_col[64 * c : 64 * c + 64, :].astype(F32)
            out_v[c] = jnp.concatenate([head4(above, c), block[0:60]], axis=0).astype(BF16)
            store_col(c)

    def send_ids_done():
        for c in send_ids:
            c.wait_recv()

    send_halos()
    progress(0)
    turn_biases()
    main_ids(jnp.zeros((24, 128), F32), range(7))
    gather_main()
    qkv_main()
    send_ids_done()
    main_ids(reg_s[...].astype(F32), range(7, 8))
    halo_ids()
    gather_halo()
    qkv_halo()
    attention()
    order_attended()
    await_weights()
    mlp(0, 368)
    send_back()
    mlp(368, 400)
    mlp(768, 384)
    finish_main()
    finish_halo()

    for c in stores:
        c.wait()
    for t in range(4):
        for c in chain(t):
            c.wait_send()
    for slot in range(1, 8):
        for kind in (0, 1):
            sib_copy(slot, kind).wait_send()
    for c in (send_col, send_cor, send_row, *send_ids, *backs):
        c.wait_send()


def block(field, region, w_qkv, w_proj, w_up, w_down, position_bias):
    vm = pltpu.VMEM
    dma = pltpu.SemaphoreType.DMA
    scratch = [
        vm((COLS, ROWS, D), BF16),
        vm((COLS, ROWS), jnp.int32),
        vm((1152, D), BF16),
        vm((1152, D), BF16),
        vm((16 * WIN_PITCH, 3 * D), BF16),
        vm((16 * WIN_PITCH, 128), BF16),
        vm((16 * WIN_PITCH, D), F32),
        vm((D, 3 * D), BF16),
        vm((D, D), BF16),
        vm((8, D, 256), BF16),
        vm((8, 256, D), BF16),
        vm((72, 128), F32),
        vm((128, 128), F32),
        vm((HEADS * 72, 128), F32),
        vm((HEADS, 72, 72), F32),
        vm((1152, D), BF16),
        vm((784, D), F32),
        vm((8, 128), F32),
        vm((24, 128), jnp.int32),
        vm((24, 128), jnp.int32),
        vm((24, 128), jnp.int32),
        vm((24, 128), jnp.int32),
        vm((80, D), BF16),
        vm((4, ROWS, D), BF16),
        vm((64, D), BF16),
        vm((16, D), BF16),
        vm((64, D), BF16),
        vm((16, D), BF16),
        vm((256, D), BF16),
        vm((64, D), BF16),
        vm((16, D), BF16),
        vm((COLS, ROWS, D), BF16),
        dma((8,)),
        dma((COLS,)),
        dma((6,)),
        dma((6,)),
        dma((3,)),
        dma((3,)),
        dma((16,)),
        dma((16,)),
        dma((14,)),
        dma((14,)),
    ]
    done = pl.pallas_call(
        kernel,
        out_shape=jax.ShapeDtypeStruct((COLS, ROWS, D), BF16),
        in_specs=[pl.BlockSpec(memory_space=pl.ANY)] * 7,
        out_specs=pl.BlockSpec(memory_space=pl.ANY),
        scratch_shapes=scratch,
        compiler_params=pltpu.CompilerParams(
            collective_id=0, has_side_effects=True, vmem_limit_bytes=58 * 1024 * 1024
        ),
    )(field.transpose(1, 0, 2), region.T, w_qkv, w_proj, w_up, w_down, position_bias)
    return done.transpose(1, 0, 2)


def solution(mesh):
    placed = (P("lat", "lon", None), P("lat", "lon"), P(), P(), P(None, "lat"), P("lat", None), P())
    return jax.shard_map(
        block, mesh=mesh, in_specs=placed, out_specs=P("lat", "lon", None), check_vma=False
    )
```

time: 103 us -> 89.5 us (0.87)
  the two profiles are of different devices: /device:TPU:31 before, /device:TPU:64 now
where the time goes in v2:
time: 89.5 us; the launch traced here: 89.3 us
  Pallas kernels  86.9 us (97%)
  local copies, waits for them, and re-layouts  2.39 us (3%)
    pallas_call x1, Pallas kernels, block(): pl.pallas_call(kernel, out_shape=jax.ShapeDtypeStruct((COLS, ROWS, D), BF...  86.9 us
    unnamed x1, local copies, waits for them, and re-layouts  2.39 us

profile of v2, /device:TPU:64, one launch (start us, length us, event | category | flops | bytes accessed | tf_op | source)
XLA Modules:
  0.0 89.3 jit_solution(13297918694829833113)
XLA Ops:
  0.0 86.9 %shard_map.73 = bf16[18,64,512]{2,1,0:T(8,128)(2,1)} custom-call(bf16[18,64,512]{2,1,0:T(8,128)(2,1)} %bitcast.4, s32[18,64]{1,0:T(8,128)} %bitcast.5, bf16[512,1536]{1,0:T(8,128)(2,1)} %wqkv_h.1, bf16[512,512]{1,0:T(8,128)(2,1)} %wproj_h.1, bf16[512,256]{1,0:T(8,128)(2,1)} %wup_h.1, bf16[256,512]{1,0:T(8,128)(2,1)} %wdown_h.1, f32[16,72,72]{2,1,0:T(8,128)} %bias_h.1), custom_call_target="tpu_custom_call" | custom-call | tf_op jit(solution)/shard_map/pallas_call | solution.py:518
  87.0 2.4 %copy.9 = bf16[64,18,512]{2,0,1:T(8,128)(2,1)} copy(bf16[64,18,512]{2,0,1:T(8,128)(2,1)} %bitcast.3) | data formatting | bytes 2359296

commit v3 on v2

--- a/solution.py
+++ b/solution.py
@@ -31,8 +31,8 @@
 
 
 def gelu(x):
-    inner = 0.7978845608028654 * (x + 0.044715 * (x * x * x))
-    return 0.5 * x * (1.0 + jnp.tanh(inner))
+    half = 0.5 * x
+    return half + half * jnp.tanh(x * (0.7978845608028654 + 0.0356774081363001 * (x * x)))
 
 
 def swap4(x):
@@ -42,21 +42,36 @@
 def kernel(
     field_h, region_h, wqkv_h, wproj_h, wup_h, wdown_h, bias_h, out_h,
     field_v, region_v, x_s, n_s, qw, idw, att, wq_v, wp_v, wu, wd,
-    braw, btmp, bias_v, bias_in, out_t, acc, hot,
+    braw, btmp, bias_v, bias_in, out_t, acc, hid, rel_in, rel_back,
     reg_out, reg_e, reg_s, reg_se, row_out, col_in, row_in, cor_in,
     back_row, back_cor, ret_col, ret_row, ret_cor, out_v,
-    local_sem, out_sem, halo_send, halo_recv, ret_send, ret_recv, w_send, w_recv, sib_send, sib_recv,
+    local_sem, out_sem, halo_send, halo_recv, ret_send, ret_recv, z_send, z_recv, xy_send, xy_recv,
+    sib_send, sib_recv, rel_send, rel_recv,
 ):
     lon = lax.axis_index("lon")
     lat = lax.axis_index("lat")
     core = lax.rem(lon, 2)
+    z_hi = lon // 32
+    x, y = lax.rem(lon // 8, 4), lax.rem(lon // 2, 4)
     west, east = lax.rem(lon + 63, 64), lax.rem(lon + 1, 64)
     north, south = lax.rem(lat + 7, 8), lax.rem(lat + 1, 8)
-    sibling = lon + 1 - 2 * core
-    far = lax.rem(lon + 32, 64)
-    z_up = (jnp.where(lat == 7, far, lon), south)
-    z_down = (jnp.where(lat == 0, far, lon), north)
-    sib = (sibling, lat)
+    half = z_hi * 32
+    other = 32 - half
+    is_first = lax.rem(lon, 32) == 0
+    is_last = lax.rem(lon, 32) == 31
+    chip = lax.rem(lon, 32) // 2
+    sib = (lon + 1 - 2 * core, lat)
+
+    def along_z(steps):
+        to = lat + steps + 16
+        return (lax.rem(z_hi + to // 8, 2) * 32 + lax.rem(lon, 32), lax.rem(to, 8))
+
+    def in_plane(to_x, to_y):
+        return (half + lax.rem(to_x, 4) * 8 + lax.rem(to_y, 4) * 2 + core, lat)
+
+    z_to = [along_z(steps) for steps in (1, -1, 2, -2, 3, -3, 4, -4)]
+    x_to = [in_plane(x + steps, y) for steps in (1, 3, 2)]
+    y_to = [in_plane(x, y + steps) for steps in (1, 3, 2)]
 
     def local(src, dst, i):
         return pltpu.make_async_copy(src, dst, local_sem.at[i])
@@ -78,57 +93,166 @@
     for c in loads:
         c.start()
 
-    partners = [(west, lat), (east, lat), (lon, north), (lon, south), (west, north), (east, south), z_up, z_down]
+    partners = [(west, lat), (east, lat), (lon, north), (lon, south), (west, north), (east, south), sib]
+    partners += z_to + x_to + y_to
     barrier = pltpu.get_barrier_semaphore()
+
+    def greet(dev):
+        pl.semaphore_signal(barrier, inc=1, device_id=dev, device_id_type=MESH)
+
+    def greet_plane(first):
+        def step(i, carry):
+            greet((first + 2 * i, lat))
+            return carry
+
+        lax.fori_loop(0, 16, step, 0)
+
     for dev in partners:
-        pl.semaphore_signal(barrier, inc=1, device_id=dev, device_id_type=MESH)
-    pl.semaphore_wait(barrier, 8)
-
-    def up(slot):
-        return wu.at[slot, pl.ds(pl.multiple_of(core * 256, 256), 256), :]
-
-    def down(slot):
-        return wd.at[slot, pl.ds(pl.multiple_of(core * 128, 128), 128), :]
-
-    def up_own():
-        return wup_h.at[pl.ds(pl.multiple_of(core * 256, 256), 256), :]
-
-    def down_own():
-        return wdown_h.at[pl.ds(pl.multiple_of(core * 128, 128), 128), :]
-
-    def chain(t):
+        greet(dev)
+
+    @pl.when(is_first)
+    def _():
+        greet_plane(other + 1)
+
+    @pl.when(is_last)
+    def _():
+        greet_plane(other)
+
+    @pl.when(jnp.logical_and(core == 0, jnp.logical_not(is_first)))
+    def _():
+        greet((half, lat))
+
+    @pl.when(jnp.logical_and(core == 1, jnp.logical_not(is_last)))
+    def _():
+        greet((half + 31, lat))
+
+    pl.semaphore_wait(barrier, len(partners) + 1 + jnp.where(jnp.logical_or(is_first, is_last), 15, 0))
+
+    z_sends = []
+    for i, dev in enumerate(z_to):
+        slot = min(i + 1, 7)
+        if i != 7:
+            z_sends.append((slot, remote(wup_h.at[x, core], wu.at[slot, x, core], z_send.at[2 * i], z_recv.at[2 * i], dev)))
+        if i != 6:
+            j = 2 * i + 1
+            z_sends.append((slot, remote(wdown_h.at[y, core], wd.at[slot, y, core], z_send.at[j], z_recv.at[j], dev)))
+    xy_sends, sib_sends = {}, {}
+    for group in range(1, 5):
+        slots = pl.ds(2 * group - 1, 2 if group < 4 else 1)
+        mine_up, mine_down = wu.at[slots, x, core], wd.at[slots, y, core]
         found = []
-        for way in (0, 1):
-            dev = (z_up, z_down)[way]
-            for kind in (0, 1):
-                if t == 3 and kind != way:
-                    continue
-                view = (up, down)[kind]
-                if t == 0:
-                    src = (up_own, down_own)[kind]()
-                else:
-                    src = view(t + 3 * way)
-                dst = view(7 if t == 3 else t + 1 + 3 * way)
-                i = t * 4 + way * 2 + kind
-                found.append(remote(src, dst, w_send.at[i], w_recv.at[i], dev))
-        return found
-
-    def sib_copy(slot, kind):
-        view = (up, down)[kind](slot)
-        i = (slot - 1) * 2 + kind
-        return remote(view, view, sib_send.at[i], sib_recv.at[i], sib)
-
-    def progress(t):
-        if t > 0:
-            for c in chain(t - 1):
+        for j in range(3):
+            i = (group - 1) * 6 + 2 * j
+            found.append(remote(mine_up, mine_up, xy_send.at[i], xy_recv.at[i], x_to[j]))
+            found.append(remote(mine_down, mine_down, xy_send.at[i + 1], xy_recv.at[i + 1], y_to[j]))
+        xy_sends[group] = found
+        found = []
+        for kind, ref in enumerate((wu, wd)):
+            i = (group - 1) * 2 + kind
+            view = ref.at[slots, :, core]
+            found.append(remote(view, view, sib_send.at[i], sib_recv.at[i], sib))
+        sib_sends[group] = found
+
+    def progress(group):
+        if group < 5:
+            for slot, c in z_sends:
+                if (slot + 1) // 2 == group:
+                    c.wait_recv()
+            for c in xy_sends[group]:
+                c.start()
+        if group > 1:
+            for c in xy_sends[group - 1]:
                 c.wait_recv()
-        if t < 4:
-            for c in chain(t):
+            for c in sib_sends[group - 1]:
                 c.start()
-        if t > 0:
-            for slot in (t, t + 3) if t < 4 else (7,):
-                for kind in (0, 1):
-                    sib_copy(slot, kind).start()
+
+    def await_weights(groups):
+        for group in groups:
+            for c in sib_sends[group]:
+                c.wait_recv()
+
+    def piece(ref, r):
+        return ref.at[r // 4, pl.ds(pl.multiple_of(lax.rem(r, 4) * 16, 16), 16)]
+
+    def push_col(r):
+        return remote(piece(field_h, r), rel_in, rel_send.at[r], rel_recv.at[0], (half + 2 * r, lat))
+
+    def rows16(ref, r):
+        return ref.at[pl.ds(pl.multiple_of(r * 16, 16), 16), :]
+
+    def push_back(r):
+        return remote(rows16(out_t, r), rel_back, rel_send.at[r], rel_recv.at[0], (half + 1 + 2 * r, lat))
+
+    own_col = remote(piece(field_h, 0), piece(col_in, 0), rel_send.at[16], halo_recv.at[0], (other + 31, lat))
+    pass_col = remote(rel_in, piece(col_in, chip), rel_send.at[16], halo_recv.at[0], (other + 31, lat))
+    own_back = remote(rows16(out_t, 15), rows16(ret_col, 15), rel_send.at[16], ret_recv.at[0], (other, lat))
+    pass_back = remote(rel_back, rows16(ret_col, chip), rel_send.at[16], ret_recv.at[0], (other, lat))
+
+    def every(low, high, act):
+        def step(r, carry):
+            act(r)
+            return carry
+
+        lax.fori_loop(low, high, step, 0)
+
+    def start_col():
+        @pl.when(is_first)
+        def _():
+            own_col.start()
+            every(1, 16, lambda r: push_col(r).start())
+
+        @pl.when(jnp.logical_not(is_first))
+        def _():
+            send_col.start()
+
+    def relay_col():
+        @pl.when(jnp.logical_and(core == 0, jnp.logical_not(is_first)))
+        def _():
+            pltpu.make_async_copy(rel_in, rel_in, rel_recv.at[0]).wait()
+            pass_col.start()
+
+    def start_back():
+        @pl.when(is_last)
+        def _():
+            own_back.start()
+            every(0, 15, lambda r: push_back(r).start())
+
+        @pl.when(jnp.logical_not(is_last))
+        def _():
+            backs[0].start()
+
+    def relay_back():
+        @pl.when(jnp.logical_and(core == 1, jnp.logical_not(is_last)))
+        def _():
+            pltpu.make_async_copy(rel_back, rel_back, rel_recv.at[0]).wait()
+            pass_back.start()
+
+    def relays_done():
+        @pl.when(is_first)
+        def _():
+            own_col.wait_send()
+            every(1, 16, lambda r: push_col(r).wait_send())
+
+        @pl.when(is_last)
+        def _():
+            own_back.wait_send()
+            every(0, 15, lambda r: push_back(r).wait_send())
+
+        @pl.when(jnp.logical_not(is_first))
+        def _():
+            send_col.wait_send()
+
+        @pl.when(jnp.logical_not(is_last))
+        def _():
+            backs[0].wait_send()
+
+        @pl.when(jnp.logical_and(core == 0, jnp.logical_not(is_first)))
+        def _():
+            pass_col.wait_send()
+
+        @pl.when(jnp.logical_and(core == 1, jnp.logical_not(is_last)))
+        def _():
+            pass_back.wait_send()
 
     send_col = remote(field_h.at[pl.ds(0, 4)], col_in, halo_send.at[0], halo_recv.at[0], (west, lat))
     send_row = remote(row_out.at[pl.ds(16, 64), :], row_in, halo_send.at[1], halo_recv.at[1], (lon, north))
@@ -139,9 +263,12 @@
         remote(reg_out, reg_se, halo_send.at[5], halo_recv.at[5], (west, north)),
     ]
     sub8 = lax.broadcasted_iota(jnp.int32, (8, D), 0)
+    scale = LOG2E * 32 ** (-0.5)
 
     def send_halos():
-        send_col.start()
+        start_col()
+        for _, c in z_sends:
+            c.start()
         loads[1].wait()
         reg_out[...] = jnp.zeros_like(reg_out)
         reg_out[0:18, 0:64] = region_v[...]
@@ -165,9 +292,7 @@
             first.append(jnp.zeros((56, 128), F32))
             btmp[...] = jnp.concatenate(first, axis=0).T
             second = [btmp[pl.ds(c, 8, stride=9), :] for c in ORDER]
-            second.append(jnp.zeros((56, 128), F32))
-            turned = jnp.concatenate(second, axis=0).T
-            bias_v[pl.ds(pl.multiple_of(h * 72, 8), 72), :] = turned[0:72] * LOG2E
+            bias_v[pl.ds(pl.multiple_of(h * 72, 8), 72), :] = jnp.concatenate(second, axis=0) * LOG2E
             return carry
 
         lax.fori_loop(0, HEADS, turn_bias, 0)
@@ -235,6 +360,7 @@
         def step(n, carry):
             lanes = pl.ds(pl.multiple_of(n * 256, 256), 256)
             res = jnp.dot(n_s[pl.ds(PAIR_AT, 784), :], wq_v[:, lanes], preferred_element_type=F32)
+            res = res * jnp.where(n < 2, scale, 1.0)
             for i in range(7):
                 scatter(lanes, i, res[PAIR_ROWS * i : PAIR_ROWS * (i + 1)])
             return carry
@@ -270,6 +396,7 @@
         def step(n, carry):
             lanes = pl.ds(pl.multiple_of(n * 256, 256), 256)
             res = jnp.dot(n_s[pl.ds(0, PAIR_AT), :], wq_v[:, lanes], preferred_element_type=F32)
+            res = res * jnp.where(n < 2, scale, 1.0)
             for i in range(2):
                 for b in range(8):
                     both = [res[64 * (2 * i + j) + 8 * b : 64 * (2 * i + j) + 8 * b + 8] for j in (0, 1)]
@@ -286,58 +413,55 @@
 
     lane256 = lax.broadcasted_iota(jnp.int32, (80, 256), 1)
     block_of = lax.rem(lane256, 128) // 32
-    low = lane256 < 128
-    zero80 = jnp.zeros((80, 256), BF16)
-    zero48 = jnp.zeros((48, 256), BF16)
-    block72 = block_of[0:72]
-    scale = LOG2E * 32 ** (-0.5)
-
-    def blocks(v):
-        return jnp.concatenate([jnp.where(low, v, zero80), zero48, jnp.where(low, zero80, v), zero48], axis=0)
 
     def window(w):
         at = pl.ds(pl.multiple_of(w * WIN_PITCH, 16), WIN_PITCH)
+        zero80 = jnp.zeros((80, 256), BF16)
+        zero128 = jnp.zeros((128, 128), BF16)
+        fill = jnp.zeros((48, D), BF16)
         ids = idw[at, :]
         wide = jnp.concatenate([ids, jnp.zeros((48, 128), BF16)], axis=0)
         same = lax.dot_general(ids, wide, NT, preferred_element_type=F32)
         shut = (same[0:72] - 1.0) * 1e30
-        halves = []
+        query = jnp.concatenate([qw[at, 0:D], fill], axis=0).T
+        value = jnp.concatenate([qw[at, 2 * D : 3 * D], fill], axis=0).T
+        outs = [None] * HEADS
         for g in range(2):
-            qg = qw[at, 256 * g : 256 * g + 256]
-            kg = qw[at, D + 256 * g : D + 256 * g + 256]
-            vg = qw[at, 2 * D + 256 * g : 2 * D + 256 * g + 256]
-            qb = jnp.concatenate([jnp.where(block_of == j, qg, zero80) for j in range(4)], axis=0)
-            scores = lax.dot_general(qb, blocks(kg), NT, preferred_element_type=F32)
-            rows = []
+            keys = qw[at, D + 256 * g : D + 256 * g + 256]
+            a, b = query[256 * g : 256 * g + 128], query[256 * g + 128 : 256 * g + 256]
+            sides = [jnp.concatenate([a, zero128], axis=1), jnp.concatenate([zero128, b], axis=1)]
+            masked = jnp.concatenate([jnp.where(block_of == j, keys, zero80) for j in range(4)], axis=0)
+            scores = jnp.dot(masked, jnp.concatenate(sides, axis=0), preferred_element_type=F32)
             for j in range(4):
-                sides = []
+                raised, sums = [], []
                 for t in range(2):
                     head = 8 * g + 4 * t + j
-                    s = scores[80 * j : 80 * j + 72, 128 * t : 128 * t + 128] * scale
+                    s = scores[80 * j : 80 * j + 72, 128 * t : 128 * t + 128]
                     s = s + bias_v[72 * head : 72 * head + 72, :] + shut
-                    ex = jnp.exp2(s - jnp.max(s, axis=-1, keepdims=True))
-                    sides.append(ex * (1.0 / jnp.sum(ex, axis=-1, keepdims=True)))
-                rows.append(jnp.concatenate(sides, axis=-1))
-                rows.append(jnp.zeros((8, 256), F32))
-            probs = jnp.concatenate(rows, axis=0).astype(BF16)
-            res = jnp.dot(probs, blocks(vg), preferred_element_type=F32)
-            o = res[0:72]
-            for j in range(1, 4):
-                o = jnp.where(block72 == j, res[80 * j : 80 * j + 72], o)
-            halves.append(o)
-        return jnp.concatenate(halves, axis=-1)
-
-    def attend_band(b, carry):
-        att[pl.ds(pl.multiple_of(2 * b * WIN_PITCH, 16), 72), :] = window(2 * b)
-        att[pl.ds(pl.multiple_of(2 * b * WIN_PITCH + WIN_PITCH, 16), 72), :] = window(2 * b + 1)
-        for t in range(1, 5):
-            @pl.when(b == 2 * t - 2)
-            def _():
-                progress(t)
+                    ex = jnp.exp2(s - jnp.max(s, axis=0, keepdims=True))
+                    sums.append(1.0 / jnp.sum(ex, axis=0, keepdims=True))
+                    raised.append(ex)
+                both = [jnp.concatenate(raised, axis=-1), jnp.zeros((8, 256), F32)]
+                probs = jnp.concatenate(both, axis=0).astype(BF16)
+                at_v = 256 * g + 32 * j
+                left = [value[at_v : at_v + 32, 0:80], value[at_v + 128 : at_v + 160, 0:80]]
+                res = jnp.dot(jnp.concatenate(left, axis=0), probs, preferred_element_type=F32)
+                outs[8 * g + j] = res[0:32, 0:128] * sums[0]
+                outs[8 * g + 4 + j] = res[32:64, 128:256] * sums[1]
+        att[pl.ds(pl.multiple_of(w * WIN_PITCH, 16), 72), :] = jnp.concatenate(outs, axis=0).T[0:72]
+
+    def attend(i, carry):
+        for u in range(4):
+            window(8 * lax.rem(i, 2) + 2 * u + i // 2)
+
+        @pl.when(i == 2)
+        def _():
+            progress(4)
+
         return carry
 
-    def attention():
-        lax.fori_loop(0, 8, attend_band, 0)
+    def attention(start, stop):
+        lax.fori_loop(start, stop, attend, 0)
 
     def attended(w, pos):
         return att[w * WIN_PITCH + 8 * pos : w * WIN_PITCH + 8 * pos + 8, :]
@@ -357,27 +481,37 @@
                 block += [attended(2 * b + s, pos) for b in range(7)]
             n_s[PAIR_AT + 112 * i : PAIR_AT + 112 * i + 112, :] = jnp.concatenate(block, axis=0).astype(BF16)
 
-    def await_weights():
-        for slot in range(1, 8):
-            for kind in (0, 1):
-                sib_copy(slot, kind).wait_recv()
-        for c in loads[4:7]:
-            c.wait()
+    def project(at):
+        mixed = x_s[at, :].astype(F32) + jnp.dot(n_s[at, :], wp_v[...], preferred_element_type=F32)
+        mixed = mixed.astype(BF16)
+        x_s[at, :] = mixed
+        n_s[at, :] = norm(mixed.astype(F32))
+
+    def raise_hidden(at, size, slots):
+        for slot in slots:
+            inner = jnp.dot(n_s[at, :], wu[slot].reshape(D, 256), preferred_element_type=F32)
+            hid[0:size, 256 * slot : 256 * slot + 256] = gelu(inner).astype(BF16)
+
+    def lower_hidden(size, low, high):
+        weights = wd[low:high].reshape(256 * (high - low), D)
+        return jnp.dot(hid[0:size, 256 * low : 256 * high], weights, preferred_element_type=F32)
+
+    def mlp_border():
+        at, size = pl.ds(0, PAIR_AT), PAIR_AT
+        project(at)
+        await_weights((1, 2))
+        raise_hidden(at, size, range(0, 5))
+        acc[...] = x_s[at, :].astype(F32) + lower_hidden(size, 0, 5)
+        progress(5)
+        await_weights((3, 4))
+        raise_hidden(at, size, range(5, 8))
+        out_t[at, :] = (acc[...] + lower_hidden(size, 5, 8)).astype(BF16)
 
     def mlp(start, size):
         at = pl.ds(start, size)
-        mixed = x_s[at, :].astype(F32) + jnp.dot(n_s[at, :], wp_v[...], preferred_element_type=F32)
-        mixed = mixed.astype(BF16).astype(F32)
-        acc[0:size, :] = mixed
-        n_s[at, :] = norm(mixed)
-
-        def hidden(s, carry):
-            h = gelu(jnp.dot(n_s[at, :], wu[s], preferred_element_type=F32)).astype(BF16)
-            acc[0:size, :] += jnp.dot(h, wd[s], preferred_element_type=F32)
-            return carry
-
-        lax.fori_loop(0, 8, hidden, 0)
-        out_t[at, :] = acc[0:size, :].astype(BF16)
+        project(at)
+        raise_hidden(at, size, range(8))
+        out_t[at, :] = (x_s[at, :].astype(F32) + lower_hidden(size, 0, 8)).astype(BF16)
 
     backs = [
         remote(out_t.at[pl.ds(0, 256), :], ret_col, ret_send.at[0], ret_recv.at[0], (east, lat)),
@@ -386,7 +520,7 @@
     ]
 
     def send_back():
-        backs[0].start()
+        start_back()
         ends = [out_t[64 * c + 48 : 64 * c + 64, :].astype(F32)[8:16] for c in range(4)]
         packed = [jnp.where(sub8 < 4, swap4(ends[2 * i]), ends[2 * i + 1]) for i in range(2)]
         back_cor[...] = jnp.concatenate(packed, axis=0).astype(BF16)
@@ -436,35 +570,41 @@
             c.wait_recv()
 
     send_halos()
-    progress(0)
     turn_biases()
+    relay_col()
+    progress(1)
     main_ids(jnp.zeros((24, 128), F32), range(7))
     gather_main()
     qkv_main()
+    progress(2)
+    attention(0, 1)
     send_ids_done()
     main_ids(reg_s[...].astype(F32), range(7, 8))
     halo_ids()
     gather_halo()
     qkv_halo()
-    attention()
+    progress(3)
+    attention(1, 4)
     order_attended()
-    await_weights()
-    mlp(0, 368)
+    for c in loads[4:7]:
+        c.wait()
+    mlp_border()
     send_back()
     mlp(368, 400)
+    relay_back()
     mlp(768, 384)
     finish_main()
     finish_halo()
 
     for c in stores:
         c.wait()
-    for t in range(4):
-        for c in chain(t):
+    relays_done()
+    for _, c in z_sends:
+        c.wait_send()
+    for group in range(1, 5):
+        for c in xy_sends[group] + sib_sends[group]:
             c.wait_send()
-    for slot in range(1, 8):
-        for kind in (0, 1):
-            sib_copy(slot, kind).wait_send()
-    for c in (send_col, send_cor, send_row, *send_ids, *backs):
+    for c in (send_cor, send_row, *send_ids, *backs[1:]):
         c.wait_send()
 
 
@@ -481,15 +621,17 @@
         vm((16 * WIN_PITCH, D), F32),
         vm((D, 3 * D), BF16),
         vm((D, D), BF16),
-        vm((8, D, 256), BF16),
-        vm((8, 256, D), BF16),
+        vm((8, 4, 2, 64, 256), BF16),
+        vm((8, 4, 2, 32, D), BF16),
         vm((72, 128), F32),
         vm((128, 128), F32),
         vm((HEADS * 72, 128), F32),
         vm((HEADS, 72, 72), F32),
         vm((1152, D), BF16),
-        vm((784, D), F32),
-        vm((8, 128), F32),
+        vm((PAIR_AT, D), F32),
+        vm((400, 2048), BF16),
+        vm((16, D), BF16),
+        vm((16, D), BF16),
         vm((24, 128), jnp.int32),
         vm((24, 128), jnp.int32),
         vm((24, 128), jnp.int32),
@@ -512,8 +654,12 @@
         dma((3,)),
         dma((16,)),
         dma((16,)),
-        dma((14,)),
-        dma((14,)),
+        dma((24,)),
+        dma((24,)),
+        dma((8,)),
+        dma((8,)),
+        dma((17,)),
+        dma((1,)),
     ]
     done = pl.pallas_call(
         kernel,
@@ -524,7 +670,10 @@
         compiler_params=pltpu.CompilerParams(
             collective_id=0, has_side_effects=True, vmem_limit_bytes=58 * 1024 * 1024
         ),
-    )(field.transpose(1, 0, 2), region.T, w_qkv, w_proj, w_up, w_down, position_bias)
+    )(
+        field.transpose(1, 0, 2), region.T, w_qkv, w_proj,
+        w_up.reshape(4, 2, 64, 256), w_down.reshape(4, 2, 32, D), position_bias,
+    )
     return done.transpose(1, 0, 2)
 
 

time: 89.5 us -> 65.9 us (0.74)
  the two profiles are of different devices: /device:TPU:64 before, /device:TPU:32 now
where the time goes in v3:
time: 65.9 us; the launch traced here: 65.8 us
  Pallas kernels  63.4 us (96%)
  local copies, waits for them, and re-layouts  2.39 us (4%)
    pallas_call x1, Pallas kernels, block(): pl.pallas_call(kernel, out_shape=jax.ShapeDtypeStruct((COLS, ROWS, D), BF...  63.4 us
    unnamed x1, local copies, waits for them, and re-layouts  2.39 us

profile of v3, /device:TPU:32, one launch (start us, length us, event | category | flops | bytes accessed | tf_op | source)
XLA Modules:
  0.0 65.8 jit_solution(7448071656156398371)
XLA Ops:
  0.0 63.4 %shard_map.73 = bf16[18,64,512]{2,1,0:T(8,128)(2,1)} custom-call(bf16[18,64,512]{2,1,0:T(8,128)(2,1)} %bitcast.6, s32[18,64]{1,0:T(8,128)} %bitcast.9, bf16[512,1536]{1,0:T(8,128)(2,1)} %wqkv_h.1, bf16[512,512]{1,0:T(8,128)(2,1)} %wproj_h.1, bf16[4,2,64,256]{3,2,1,0:T(8,128)(2,1)} %bitcast.7, bf16[4,2,32,512]{3,2,1,0:T(8,128)(2,1)} %bitcast.8, ...), custom_call_target="tpu_custom_call" | custom-call | tf_op jit(solution)/shard_map/pallas_call | solution.py:664
  63.4 2.4 %copy.9 = bf16[64,18,512]{2,0,1:T(8,128)(2,1)} copy(bf16[64,18,512]{2,0,1:T(8,128)(2,1)} %bitcast.5) | data formatting | bytes 2359296

commit v4 on v3

--- a/solution.py
+++ b/solution.py
@@ -42,7 +42,7 @@
 def kernel(
     field_h, region_h, wqkv_h, wproj_h, wup_h, wdown_h, bias_h, out_h,
     field_v, region_v, x_s, n_s, qw, idw, att, wq_v, wp_v, wu, wd,
-    braw, btmp, bias_v, bias_in, out_t, acc, hid, rel_in, rel_back,
+    braw, btmp, bias_v, bias_in, out_t, x_e, acc, hid, rel_in, rel_back,
     reg_out, reg_e, reg_s, reg_se, row_out, col_in, row_in, cor_in,
     back_row, back_cor, ret_col, ret_row, ret_cor, out_v,
     local_sem, out_sem, halo_send, halo_recv, ret_send, ret_recv, z_send, z_recv, xy_send, xy_recv,
@@ -153,17 +153,19 @@
             found.append(remote(view, view, sib_send.at[i], sib_recv.at[i], sib))
         sib_sends[group] = found
 
-    def progress(group):
-        if group < 5:
+    def spread(groups):
+        for group in groups:
             for slot, c in z_sends:
                 if (slot + 1) // 2 == group:
                     c.wait_recv()
             for c in xy_sends[group]:
                 c.start()
-        if group > 1:
-            for c in xy_sends[group - 1]:
+
+    def share(groups):
+        for group in groups:
+            for c in xy_sends[group]:
                 c.wait_recv()
-            for c in sib_sends[group - 1]:
+            for c in sib_sends[group]:
                 c.start()
 
     def await_weights(groups):
@@ -181,11 +183,11 @@
         return ref.at[pl.ds(pl.multiple_of(r * 16, 16), 16), :]
 
     def push_back(r):
-        return remote(rows16(out_t, r), rel_back, rel_send.at[r], rel_recv.at[0], (half + 1 + 2 * r, lat))
+        return remote(rows16(x_s, r), rel_back, rel_send.at[r], rel_recv.at[0], (half + 1 + 2 * r, lat))
 
     own_col = remote(piece(field_h, 0), piece(col_in, 0), rel_send.at[16], halo_recv.at[0], (other + 31, lat))
     pass_col = remote(rel_in, piece(col_in, chip), rel_send.at[16], halo_recv.at[0], (other + 31, lat))
-    own_back = remote(rows16(out_t, 15), rows16(ret_col, 15), rel_send.at[16], ret_recv.at[0], (other, lat))
+    own_back = remote(rows16(x_s, 15), rows16(ret_col, 15), rel_send.at[16], ret_recv.at[0], (other, lat))
     pass_back = remote(rel_back, rows16(ret_col, chip), rel_send.at[16], ret_recv.at[0], (other, lat))
 
     def every(low, high, act):
@@ -267,7 +269,7 @@
 
     def send_halos():
         start_col()
-        for _, c in z_sends:
+        for _, c in z_sends[0:8]:
             c.start()
         loads[1].wait()
         reg_out[...] = jnp.zeros_like(reg_out)
@@ -360,7 +362,6 @@
         def step(n, carry):
             lanes = pl.ds(pl.multiple_of(n * 256, 256), 256)
             res = jnp.dot(n_s[pl.ds(PAIR_AT, 784), :], wq_v[:, lanes], preferred_element_type=F32)
-            res = res * jnp.where(n < 2, scale, 1.0)
             for i in range(7):
                 scatter(lanes, i, res[PAIR_ROWS * i : PAIR_ROWS * (i + 1)])
             return carry
@@ -396,7 +397,6 @@
         def step(n, carry):
             lanes = pl.ds(pl.multiple_of(n * 256, 256), 256)
             res = jnp.dot(n_s[pl.ds(0, PAIR_AT), :], wq_v[:, lanes], preferred_element_type=F32)
-            res = res * jnp.where(n < 2, scale, 1.0)
             for i in range(2):
                 for b in range(8):
                     both = [res[64 * (2 * i + j) + 8 * b : 64 * (2 * i + j) + 8 * b + 8] for j in (0, 1)]
@@ -436,7 +436,7 @@
                 raised, sums = [], []
                 for t in range(2):
                     head = 8 * g + 4 * t + j
-                    s = scores[80 * j : 80 * j + 72, 128 * t : 128 * t + 128]
+                    s = scores[80 * j : 80 * j + 72, 128 * t : 128 * t + 128] * scale
                     s = s + bias_v[72 * head : 72 * head + 72, :] + shut
                     ex = jnp.exp2(s - jnp.max(s, axis=0, keepdims=True))
                     sums.append(1.0 / jnp.sum(ex, axis=0, keepdims=True))
@@ -453,11 +453,6 @@
     def attend(i, carry):
         for u in range(4):
             window(8 * lax.rem(i, 2) + 2 * u + i // 2)
-
-        @pl.when(i == 2)
-        def _():
-            progress(4)
-
         return carry
 
     def attention(start, stop):
@@ -466,10 +461,12 @@
     def attended(w, pos):
         return att[w * WIN_PITCH + 8 * pos : w * WIN_PITCH + 8 * pos + 8, :]
 
-    def order_attended():
+    def order_halo():
         for c in range(4):
             block = [attended(2 * b + 1, c) for b in range(8)]
             n_s[64 * c : 64 * c + 64, :] = jnp.concatenate(block, axis=0).astype(BF16)
+
+    def order_main():
         block = [att[14 * WIN_PITCH : 14 * WIN_PITCH + 72, :], att[15 * WIN_PITCH + 32 : 15 * WIN_PITCH + 72, :]]
         n_s[LAST_AT:PAIR_AT, :] = jnp.concatenate(block, axis=0).astype(BF16)
         for i, pair in enumerate(PAIRS):
@@ -481,11 +478,12 @@
                 block += [attended(2 * b + s, pos) for b in range(7)]
             n_s[PAIR_AT + 112 * i : PAIR_AT + 112 * i + 112, :] = jnp.concatenate(block, axis=0).astype(BF16)
 
-    def project(at):
+    def project(start, size):
+        at = pl.ds(start, size)
         mixed = x_s[at, :].astype(F32) + jnp.dot(n_s[at, :], wp_v[...], preferred_element_type=F32)
         mixed = mixed.astype(BF16)
         x_s[at, :] = mixed
-        n_s[at, :] = norm(mixed.astype(F32))
+        return mixed
 
     def raise_hidden(at, size, slots):
         for slot in slots:
@@ -496,36 +494,42 @@
         weights = wd[low:high].reshape(256 * (high - low), D)
         return jnp.dot(hid[0:size, 256 * low : 256 * high], weights, preferred_element_type=F32)
 
-    def mlp_border():
+    def mlp_near(start, size):
+        at = pl.ds(start, size)
+        n_s[at, :] = norm(project(start, size).astype(F32))
+        raise_hidden(at, size, range(0, 5))
+        acc[start - PAIR_AT : start - PAIR_AT + size, :] = x_s[at, :].astype(F32) + lower_hidden(size, 0, 5)
+
+    def mlp_far(start, size):
+        at = pl.ds(start, size)
+        raise_hidden(at, size, range(5, 8))
+        total = acc[start - PAIR_AT : start - PAIR_AT + size, :] + lower_hidden(size, 5, 8)
+        out_t[at, :] = total.astype(BF16)
+
+    def mlp_edge():
         at, size = pl.ds(0, PAIR_AT), PAIR_AT
-        project(at)
-        await_weights((1, 2))
-        raise_hidden(at, size, range(0, 5))
-        acc[...] = x_s[at, :].astype(F32) + lower_hidden(size, 0, 5)
-        progress(5)
-        await_weights((3, 4))
-        raise_hidden(at, size, range(5, 8))
-        out_t[at, :] = (acc[...] + lower_hidden(size, 5, 8)).astype(BF16)
-
-    def mlp(start, size):
-        at = pl.ds(start, size)
-        project(at)
         raise_hidden(at, size, range(8))
-        out_t[at, :] = (x_s[at, :].astype(F32) + lower_hidden(size, 0, 8)).astype(BF16)
+        out_t[at, :] = (x_e[...].astype(F32) + lower_hidden(size, 0, 8)).astype(BF16)
 
     backs = [
-        remote(out_t.at[pl.ds(0, 256), :], ret_col, ret_send.at[0], ret_recv.at[0], (east, lat)),
+        remote(x_s.at[pl.ds(0, 256), :], ret_col, ret_send.at[0], ret_recv.at[0], (east, lat)),
         remote(back_cor, ret_cor, ret_send.at[1], ret_recv.at[1], (east, south)),
         remote(back_row, ret_row, ret_send.at[2], ret_recv.at[2], (lon, south)),
     ]
 
-    def send_back():
+    def send_back_cols():
+        loads[4].wait()
+        order_halo()
+        project(0, 256)
         start_back()
-        ends = [out_t[64 * c + 48 : 64 * c + 64, :].astype(F32)[8:16] for c in range(4)]
+        ends = [x_s[64 * c + 48 : 64 * c + 64, :].astype(F32)[8:16] for c in range(4)]
         packed = [jnp.where(sub8 < 4, swap4(ends[2 * i]), ends[2 * i + 1]) for i in range(2)]
         back_cor[...] = jnp.concatenate(packed, axis=0).astype(BF16)
         backs[1].start()
-        last = out_t[LAST_AT:PAIR_AT, :].astype(F32)
+
+    def send_back_rows():
+        order_main()
+        last = project(LAST_AT, PAIR_ROWS).astype(F32)
         packed = []
         for i in range(7):
             packed.append(jnp.where(sub8 < 4, swap4(last[16 * i : 16 * i + 8]), last[16 * i + 8 : 16 * i + 16]))
@@ -544,26 +548,37 @@
         piece = packed[8 * (i // 2) : 8 * (i // 2) + 8]
         return piece[0:4] if i % 2 == 0 else piece[4:8]
 
-    def finish_main():
+    def take_back():
         backs[2].wait_recv()
         above = ret_row[...].astype(F32)
-        last = out_t[LAST_AT:PAIR_AT, :].astype(F32)
+        last = x_s[LAST_AT:PAIR_AT, :].astype(F32)
+        block = []
+        for k in range(14):
+            block += [last[8 * k : 8 * k + 4], head4(above, k)]
+        block = jnp.concatenate(block, axis=0)
+        x_e[LAST_AT:PAIR_AT, :] = block.astype(BF16)
+        n_s[LAST_AT:PAIR_AT, :] = norm(block)
+        backs[1].wait_recv()
+        above = ret_cor[...].astype(F32)
+        backs[0].wait_recv()
+        for c in range(4):
+            block = jnp.concatenate([ret_col[64 * c : 64 * c + 64, :].astype(F32)[0:60], head4(above, c)], axis=0)
+            x_e[64 * c : 64 * c + 64, :] = block.astype(BF16)
+            n_s[64 * c : 64 * c + 64, :] = norm(block)
+
+    def finish():
+        for c in range(4):
+            block = out_t[64 * c : 64 * c + 64, :].astype(F32)
+            out_v[c] = jnp.concatenate([block[60:64], block[0:60]], axis=0).astype(BF16)
+            store_col(c)
+        ends = out_t[LAST_AT:PAIR_AT, :].astype(F32)
         for i, pair in enumerate(PAIRS):
             block = out_t[PAIR_AT + 112 * i : PAIR_AT + 112 * i + 112, :].astype(F32)
             for j, c in enumerate(pair):
                 k = LAST.index(c)
-                parts = [head4(above, k), block[56 * j : 56 * j + 56], last[8 * k : 8 * k + 4]]
+                parts = [ends[8 * k + 4 : 8 * k + 8], block[56 * j : 56 * j + 56], ends[8 * k : 8 * k + 4]]
                 out_v[c + 4] = jnp.concatenate(parts, axis=0).astype(BF16)
                 store_col(c + 4)
-
-    def finish_halo():
-        backs[1].wait_recv()
-        above = ret_cor[...].astype(F32)
-        backs[0].wait_recv()
-        for c in range(4):
-            block = ret_col[64 * c : 64 * c + 64, :].astype(F32)
-            out_v[c] = jnp.concatenate([head4(above, c), block[0:60]], axis=0).astype(BF16)
-            store_col(c)
 
     def send_ids_done():
         for c in send_ids:
@@ -571,30 +586,39 @@
 
     send_halos()
     turn_biases()
+    for _, c in z_sends[8:]:
+        c.start()
     relay_col()
-    progress(1)
     main_ids(jnp.zeros((24, 128), F32), range(7))
     gather_main()
     qkv_main()
-    progress(2)
+    spread((1, 2))
     attention(0, 1)
     send_ids_done()
     main_ids(reg_s[...].astype(F32), range(7, 8))
     halo_ids()
     gather_halo()
     qkv_halo()
-    progress(3)
-    attention(1, 4)
-    order_attended()
-    for c in loads[4:7]:
+    attention(2, 3)
+    spread((3, 4))
+    attention(3, 4)
+    share((1, 2))
+    send_back_cols()
+    attention(1, 2)
+    send_back_rows()
+    relay_back()
+    share((3, 4))
+    for c in loads[5:7]:
         c.wait()
-    mlp_border()
-    send_back()
-    mlp(368, 400)
-    relay_back()
-    mlp(768, 384)
-    finish_main()
-    finish_halo()
+    await_weights((1, 2))
+    mlp_near(368, 400)
+    mlp_near(768, 384)
+    await_weights((3, 4))
+    mlp_far(368, 400)
+    mlp_far(768, 384)
+    take_back()
+    mlp_edge()
+    finish()
 
     for c in stores:
         c.wait()
@@ -628,8 +652,9 @@
         vm((HEADS * 72, 128), F32),
         vm((HEADS, 72, 72), F32),
         vm((1152, D), BF16),
-        vm((PAIR_AT, D), F32),
-        vm((400, 2048), BF16),
+        vm((PAIR_AT, D), BF16),
+        vm((784, D), F32),
+        vm((784, 2048), BF16),
         vm((16, D), BF16),
         vm((16, D), BF16),
         vm((24, 128), jnp.int32),

time: 65.9 us -> 62.4 us (0.947)
  Pallas kernels: 63.4 us -> 59.9 us
    pallas_call x1, Pallas kernels: 63.4 us -> 59.9 us  [block(): pl.pallas_call(kernel, out_shape=jax.ShapeDtypeStruct((COLS, ROWS, D), BF...]
where the time goes in v4:
time: 62.4 us; the launch traced here: 62.3 us
  Pallas kernels  59.9 us (96%)
  local copies, waits for them, and re-layouts  2.39 us (4%)
    pallas_call x1, Pallas kernels, block(): pl.pallas_call(kernel, out_shape=jax.ShapeDtypeStruct((COLS, ROWS, D), BF...  59.9 us
    unnamed x1, local copies, waits for them, and re-layouts  2.39 us

profile of v4, /device:TPU:32, one launch (start us, length us, event | category | flops | bytes accessed | tf_op | source)
XLA Modules:
  0.0 62.3 jit_solution(5611461672007604194)
XLA Ops:
  0.0 59.9 %shard_map.73 = bf16[18,64,512]{2,1,0:T(8,128)(2,1)} custom-call(bf16[18,64,512]{2,1,0:T(8,128)(2,1)} %bitcast.6, s32[18,64]{1,0:T(8,128)} %bitcast.9, bf16[512,1536]{1,0:T(8,128)(2,1)} %wqkv_h.1, bf16[512,512]{1,0:T(8,128)(2,1)} %wproj_h.1, bf16[4,2,64,256]{3,2,1,0:T(8,128)(2,1)} %bitcast.7, bf16[4,2,32,512]{3,2,1,0:T(8,128)(2,1)} %bitcast.8, ...), custom_call_target="tpu_custom_call" | custom-call | tf_op jit(solution)/shard_map/pallas_call | solution.py:689
  59.9 2.4 %copy.9 = bf16[64,18,512]{2,0,1:T(8,128)(2,1)} copy(bf16[64,18,512]{2,0,1:T(8,128)(2,1)} %bitcast.5) | data formatting | bytes 2359296

commit v5 on v4

--- a/solution.py
+++ b/solution.py
@@ -42,11 +42,12 @@
 def kernel(
     field_h, region_h, wqkv_h, wproj_h, wup_h, wdown_h, bias_h, out_h,
     field_v, region_v, x_s, n_s, qw, idw, att, wq_v, wp_v, wu, wd,
-    braw, btmp, bias_v, bias_in, out_t, x_e, acc, hid, rel_in, rel_back,
+    braw, btmp, bias_v, bias_in, out_t, x_e, acc, hid, rel_in, rel_far,
+    far_in, far_row, reg_f, reg_fs, far_cor, x_f, n_f,
     reg_out, reg_e, reg_s, reg_se, row_out, col_in, row_in, cor_in,
     back_row, back_cor, ret_col, ret_row, ret_cor, out_v,
     local_sem, out_sem, halo_send, halo_recv, ret_send, ret_recv, z_send, z_recv, xy_send, xy_recv,
-    sib_send, sib_recv, rel_send, rel_recv,
+    sib_send, sib_recv, rel_send, rel_recv, far_send, far_recv,
 ):
     lon = lax.axis_index("lon")
     lat = lax.axis_index("lat")
@@ -93,40 +94,44 @@
     for c in loads:
         c.start()
 
-    partners = [(west, lat), (east, lat), (lon, north), (lon, south), (west, north), (east, south), sib]
+    partners = [(west, lat), (east, lat), (lon, north), (lon, south), (west, north), (east, south), (west, south), sib]
     partners += z_to + x_to + y_to
     barrier = pltpu.get_barrier_semaphore()
 
     def greet(dev):
         pl.semaphore_signal(barrier, inc=1, device_id=dev, device_id_type=MESH)
 
-    def greet_plane(first):
+    def greet_plane(first, count):
         def step(i, carry):
             greet((first + 2 * i, lat))
             return carry
 
-        lax.fori_loop(0, 16, step, 0)
+        lax.fori_loop(0, count, step, 0)
 
     for dev in partners:
         greet(dev)
+    near_relay = jnp.logical_and(core == 0, jnp.logical_not(is_first))
+    far_relay = jnp.logical_and(core == 1, chip < 10)
 
     @pl.when(is_first)
     def _():
-        greet_plane(other + 1)
+        greet_plane(other + 1, 10)
 
     @pl.when(is_last)
     def _():
-        greet_plane(other)
-
-    @pl.when(jnp.logical_and(core == 0, jnp.logical_not(is_first)))
+        greet_plane(other, 16)
+
+    @pl.when(near_relay)
     def _():
         greet((half, lat))
 
-    @pl.when(jnp.logical_and(core == 1, jnp.logical_not(is_last)))
+    @pl.when(far_relay)
     def _():
         greet((half + 31, lat))
 
-    pl.semaphore_wait(barrier, len(partners) + 1 + jnp.where(jnp.logical_or(is_first, is_last), 15, 0))
+    more = jnp.where(jnp.logical_or(core == 0, far_relay), 1, 0)
+    more = more + jnp.where(is_first, 15, 0) + jnp.where(is_last, 10, 0)
+    pl.semaphore_wait(barrier, len(partners) + more)
 
     z_sends = []
     for i, dev in enumerate(z_to):
@@ -176,19 +181,26 @@
     def piece(ref, r):
         return ref.at[r // 4, pl.ds(pl.multiple_of(lax.rem(r, 4) * 16, 16), 16)]
 
+    def far_piece(ref, first, r):
+        return ref.at[first + r // 2, pl.ds(pl.multiple_of(lax.rem(r, 2) * 32, 32), 32)]
+
     def push_col(r):
         return remote(piece(field_h, r), rel_in, rel_send.at[r], rel_recv.at[0], (half + 2 * r, lat))
 
-    def rows16(ref, r):
-        return ref.at[pl.ds(pl.multiple_of(r * 16, 16), 16), :]
-
-    def push_back(r):
-        return remote(rows16(x_s, r), rel_back, rel_send.at[r], rel_recv.at[0], (half + 1 + 2 * r, lat))
+    def push_far(r):
+        return remote(far_piece(field_h, 13, r), rel_far, rel_send.at[r], rel_recv.at[0], (half + 1 + 2 * r, lat))
 
     own_col = remote(piece(field_h, 0), piece(col_in, 0), rel_send.at[16], halo_recv.at[0], (other + 31, lat))
     pass_col = remote(rel_in, piece(col_in, chip), rel_send.at[16], halo_recv.at[0], (other + 31, lat))
-    own_back = remote(rows16(x_s, 15), rows16(ret_col, 15), rel_send.at[16], ret_recv.at[0], (other, lat))
-    pass_back = remote(rel_back, rows16(ret_col, chip), rel_send.at[16], ret_recv.at[0], (other, lat))
+    near_chip = jnp.where(far_relay, chip, 0)
+    pass_far = remote(rel_far, far_piece(far_in, 0, near_chip), rel_send.at[16], far_recv.at[0], (other, lat))
+    far_sends = [
+        remote(reg_out, reg_f, far_send.at[0], far_recv.at[1], (other, lat)),
+        remote(reg_out, reg_fs, far_send.at[1], far_recv.at[2], (other, north)),
+        remote(row_out.at[pl.ds(48, 32), :], far_row, far_send.at[2], far_recv.at[3], (other, north)),
+    ]
+    pass_far_all = remote(far_in, far_in, far_send.at[0], far_recv.at[0], (other, lat))
+    far_back = remote(far_cor, ret_cor, far_send.at[3], ret_recv.at[1], (lon, south))
 
     def every(low, high, act):
         def step(r, carry):
@@ -207,57 +219,59 @@
         def _():
             send_col.start()
 
-    def relay_col():
-        @pl.when(jnp.logical_and(core == 0, jnp.logical_not(is_first)))
+        @pl.when(is_last)
+        def _():
+            every(0, 10, lambda r: push_far(r).start())
+
+    def relay():
+        @pl.when(near_relay)
         def _():
             pltpu.make_async_copy(rel_in, rel_in, rel_recv.at[0]).wait()
             pass_col.start()
 
+        @pl.when(far_relay)
+        def _():
+            pltpu.make_async_copy(rel_far, rel_far, rel_recv.at[0]).wait()
+            pass_far.start()
+
     def start_back():
-        @pl.when(is_last)
-        def _():
-            own_back.start()
-            every(0, 15, lambda r: push_back(r).start())
-
         @pl.when(jnp.logical_not(is_last))
         def _():
             backs[0].start()
-
-    def relay_back():
-        @pl.when(jnp.logical_and(core == 1, jnp.logical_not(is_last)))
-        def _():
-            pltpu.make_async_copy(rel_back, rel_back, rel_recv.at[0]).wait()
-            pass_back.start()
+            backs[1].start()
 
     def relays_done():
         @pl.when(is_first)
         def _():
             own_col.wait_send()
             every(1, 16, lambda r: push_col(r).wait_send())
+            far_back.wait_send()
+
+        @pl.when(jnp.logical_not(is_first))
+        def _():
+            send_col.wait_send()
 
         @pl.when(is_last)
         def _():
-            own_back.wait_send()
-            every(0, 15, lambda r: push_back(r).wait_send())
-
-        @pl.when(jnp.logical_not(is_first))
-        def _():
-            send_col.wait_send()
+            every(0, 10, lambda r: push_far(r).wait_send())
+            for c in far_sends:
+                c.wait_send()
 
         @pl.when(jnp.logical_not(is_last))
         def _():
             backs[0].wait_send()
-
-        @pl.when(jnp.logical_and(core == 0, jnp.logical_not(is_first)))
+            backs[1].wait_send()
+
+        @pl.when(near_relay)
         def _():
             pass_col.wait_send()
 
-        @pl.when(jnp.logical_and(core == 1, jnp.logical_not(is_last)))
-        def _():
-            pass_back.wait_send()
+        @pl.when(far_relay)
+        def _():
+            pass_far.wait_send()
 
     send_col = remote(field_h.at[pl.ds(0, 4)], col_in, halo_send.at[0], halo_recv.at[0], (west, lat))
-    send_row = remote(row_out.at[pl.ds(16, 64), :], row_in, halo_send.at[1], halo_recv.at[1], (lon, north))
+    send_row = remote(row_out, row_in, halo_send.at[1], halo_recv.at[1], (lon, north))
     send_cor = remote(row_out.at[pl.ds(0, 16), :], cor_in, halo_send.at[2], halo_recv.at[2], (west, north))
     send_ids = [
         remote(reg_out, reg_e, halo_send.at[3], halo_recv.at[3], (west, lat)),
@@ -276,6 +290,12 @@
         reg_out[0:18, 0:64] = region_v[...]
         for c in send_ids:
             c.start()
+
+        @pl.when(is_last)
+        def _():
+            for c in far_sends[0:2]:
+                c.start()
+
         loads[0].wait()
         tops = [field_v[c, 0:16, :].astype(F32)[0:8] for c in range(COLS)]
         packed = [jnp.where(sub8 < 4, tops[2 * i], swap4(tops[2 * i + 1])) for i in range(9)]
@@ -283,6 +303,10 @@
         row_out[...] = jnp.concatenate(packed, axis=0).astype(BF16)
         send_row.start()
         send_cor.start()
+
+        @pl.when(is_last)
+        def _():
+            far_sends[2].start()
 
     def turn_biases():
         loads[2].wait()
@@ -311,10 +335,13 @@
         wide = jnp.broadcast_to(table[:, c : c + 1], (64, 128))
         return (wide == lane64.astype(F32)).astype(F32)
 
+    def window_of(b, s):
+        return 2 * b + s if s < 2 else 16 + b
+
     def put_ids(s, pos, top, low, bands):
         for b in bands:
             rows = [top[8 * b : 8 * b + 8], low[8 * b : 8 * b + 8]]
-            idw[pl.ds((2 * b + s) * WIN_PITCH + 16 * pos, 16), :] = jnp.concatenate(rows, axis=0).astype(BF16)
+            idw[pl.ds(window_of(b, s) * WIN_PITCH + 16 * pos, 16), :] = jnp.concatenate(rows, axis=0).astype(BF16)
 
     def main_ids(below, bands):
         table = id_rows(reg_out[...].astype(F32), below)
@@ -328,6 +355,15 @@
                 put_ids(1, 4, second, zero, bands)
             else:
                 put_ids(1, i - 3, first, second, bands)
+
+    def far_ids():
+        table = id_rows(reg_out[...].astype(F32), reg_s[...].astype(F32))
+        for i in (0, 1):
+            put_ids(2, i, hot_col(table, 2 * i), hot_col(table, 2 * i + 1), range(8))
+        table = id_rows(reg_f[...].astype(F32), reg_fs[...].astype(F32))
+        put_ids(2, 2, hot_col(table, 13), hot_col(table, 14), range(8))
+        put_ids(2, 3, hot_col(table, 15), hot_col(table, 16), range(8))
+        put_ids(2, 4, hot_col(table, 17), jnp.zeros((64, 128), F32), range(8))
 
     def halo_ids():
         table = id_rows(reg_e[...].astype(F32), reg_se[...].astype(F32))
@@ -356,24 +392,12 @@
                 both = jnp.concatenate([first, second], axis=0).astype(BF16)
                 qw[pl.ds((2 * b + s) * WIN_PITCH + 16 * pos, 16), lanes] = both
 
-    def qkv_main():
-        loads[3].wait()
-
-        def step(n, carry):
-            lanes = pl.ds(pl.multiple_of(n * 256, 256), 256)
-            res = jnp.dot(n_s[pl.ds(PAIR_AT, 784), :], wq_v[:, lanes], preferred_element_type=F32)
-            for i in range(7):
-                scatter(lanes, i, res[PAIR_ROWS * i : PAIR_ROWS * (i + 1)])
-            return carry
-
-        lax.fori_loop(0, 6, step, 0)
-
-    def gather_halo():
+    def gather_last():
         send_row.wait_recv()
         below = row_in[...].astype(F32)
         ready = {}
         for c in range(14):
-            piece = below[8 * (c // 2) : 8 * (c // 2) + 8]
+            piece = below[16 + 8 * (c // 2) : 24 + 8 * (c // 2)]
             if c % 2 == 0:
                 piece = swap4(piece)
             mine = swap4(field_v[c + 4, 48:64, :].astype(F32)[8:16])
@@ -382,6 +406,24 @@
         at = pl.ds(LAST_AT, PAIR_ROWS)
         x_s[at, :] = block.astype(BF16)
         n_s[at, :] = norm(block)
+
+    def qkv_main():
+        loads[3].wait()
+
+        def step(n, carry):
+            lanes = pl.ds(pl.multiple_of(n * 256, 256), 256)
+            res = jnp.dot(n_s[pl.ds(LAST_AT, 896), :], wq_v[:, lanes], preferred_element_type=F32)
+            for i in range(7):
+                scatter(lanes, i, res[PAIR_ROWS * (i + 1) : PAIR_ROWS * (i + 2)])
+            last = res[0:PAIR_ROWS]
+            fill = jnp.zeros((8, 256), F32)
+            qw[pl.ds(14 * WIN_PITCH, 80), lanes] = jnp.concatenate([last[0:72], fill], axis=0).astype(BF16)
+            qw[pl.ds(15 * WIN_PITCH + 32, 48), lanes] = jnp.concatenate([last[72:112], fill], axis=0).astype(BF16)
+            return carry
+
+        lax.fori_loop(0, 6, step, 0)
+
+    def gather_halo():
         send_cor.wait_recv()
         corner = cor_in[...].astype(F32)
         send_col.wait_recv()
@@ -396,17 +438,12 @@
     def qkv_halo():
         def step(n, carry):
             lanes = pl.ds(pl.multiple_of(n * 256, 256), 256)
-            res = jnp.dot(n_s[pl.ds(0, PAIR_AT), :], wq_v[:, lanes], preferred_element_type=F32)
+            res = jnp.dot(n_s[pl.ds(0, LAST_AT), :], wq_v[:, lanes], preferred_element_type=F32)
             for i in range(2):
                 for b in range(8):
                     both = [res[64 * (2 * i + j) + 8 * b : 64 * (2 * i + j) + 8 * b + 8] for j in (0, 1)]
                     at = pl.ds((2 * b + 1) * WIN_PITCH + 16 * i, 16)
                     qw[at, lanes] = jnp.concatenate(both, axis=0).astype(BF16)
-            last = res[LAST_AT:PAIR_AT]
-            fill = jnp.zeros((8, 256), F32)
-            qw[pl.ds(14 * WIN_PITCH, 80), lanes] = jnp.concatenate([last[0:72], fill], axis=0).astype(BF16)
-            tail = [last[72:104], last[104:112], fill]
-            qw[pl.ds(15 * WIN_PITCH + 32, 48), lanes] = jnp.concatenate(tail, axis=0).astype(BF16)
             return carry
 
         lax.fori_loop(0, 6, step, 0)
@@ -452,7 +489,7 @@
 
     def attend(i, carry):
         for u in range(4):
-            window(8 * lax.rem(i, 2) + 2 * u + i // 2)
+            window(jnp.where(i < 4, 8 * lax.rem(i, 2) + 2 * u + i // 2, 4 * i + u))
         return carry
 
     def attention(start, stop):
@@ -461,10 +498,10 @@
     def attended(w, pos):
         return att[w * WIN_PITCH + 8 * pos : w * WIN_PITCH + 8 * pos + 8, :]
 
-    def order_halo():
+    def order_halo(ref, s):
         for c in range(4):
-            block = [attended(2 * b + 1, c) for b in range(8)]
-            n_s[64 * c : 64 * c + 64, :] = jnp.concatenate(block, axis=0).astype(BF16)
+            block = [attended(window_of(b, s), c) for b in range(8)]
+            ref[64 * c : 64 * c + 64, :] = jnp.concatenate(block, axis=0).astype(BF16)
 
     def order_main():
         block = [att[14 * WIN_PITCH : 14 * WIN_PITCH + 72, :], att[15 * WIN_PITCH + 32 : 15 * WIN_PITCH + 72, :]]
@@ -517,15 +554,59 @@
         remote(back_row, ret_row, ret_send.at[2], ret_recv.at[2], (lon, south)),
     ]
 
+    def pack_ends(ref):
+        ends = [ref[64 * c + 48 : 64 * c + 64, :].astype(F32)[8:16] for c in range(4)]
+        packed = [jnp.where(sub8 < 4, swap4(ends[2 * i]), ends[2 * i + 1]) for i in range(2)]
+        return jnp.concatenate(packed, axis=0).astype(BF16)
+
     def send_back_cols():
         loads[4].wait()
-        order_halo()
+        order_halo(n_s, 1)
         project(0, 256)
+        back_cor[...] = pack_ends(x_s)
         start_back()
-        ends = [x_s[64 * c + 48 : 64 * c + 64, :].astype(F32)[8:16] for c in range(4)]
-        packed = [jnp.where(sub8 < 4, swap4(ends[2 * i]), ends[2 * i + 1]) for i in range(2)]
-        back_cor[...] = jnp.concatenate(packed, axis=0).astype(BF16)
-        backs[1].start()
+
+    def far_rows(packed, i):
+        piece = packed[8 * (i // 2) : 8 * (i // 2) + 8]
+        return piece[0:4] if i % 2 == 0 else piece[4:8]
+
+    def far_work():
+        for c in (*far_sends, pass_far_all):
+            c.wait_recv()
+        far_ids()
+        below = row_in[0:16, :].astype(F32)
+        for c in range(4):
+            block = jnp.concatenate([field_v[c].astype(F32)[4:64], far_rows(below, c)], axis=0)
+            x_f[64 * c : 64 * c + 64, :] = block.astype(BF16)
+            n_f[64 * c : 64 * c + 64, :] = norm(block)
+        below = far_row[...].astype(F32)
+        for k in range(5):
+            block = jnp.concatenate([far_in[k].astype(F32)[4:64], far_rows(below, k + 1)], axis=0)
+            n_f[256 + 64 * k : 320 + 64 * k, :] = norm(block)
+
+        def step(n, carry):
+            lanes = pl.ds(pl.multiple_of(n * 256, 256), 256)
+            res = jnp.dot(n_f[...], wq_v[:, lanes], preferred_element_type=F32)
+            for i in range(5):
+                for b in range(8):
+                    first = res[128 * i + 8 * b : 128 * i + 8 * b + 8]
+                    second = res[128 * i + 64 + 8 * b : 128 * i + 72 + 8 * b] if i < 4 else jnp.zeros_like(first)
+                    at = pl.ds((16 + b) * WIN_PITCH + 16 * i, 16)
+                    qw[at, lanes] = jnp.concatenate([first, second], axis=0).astype(BF16)
+            return carry
+
+        lax.fori_loop(0, 6, step, 0)
+        attention(4, 6)
+        order_halo(n_f, 2)
+        mixed = x_f[...].astype(F32) + jnp.dot(n_f[0:256, :], wp_v[...], preferred_element_type=F32)
+        ret_col[...] = mixed.astype(BF16)
+        far_cor[...] = pack_ends(ret_col)
+        far_back.start()
+
+    def far_windows():
+        @pl.when(is_first)
+        def _():
+            far_work()
 
     def send_back_rows():
         order_main()
@@ -560,7 +641,11 @@
         n_s[LAST_AT:PAIR_AT, :] = norm(block)
         backs[1].wait_recv()
         above = ret_cor[...].astype(F32)
-        backs[0].wait_recv()
+
+        @pl.when(jnp.logical_not(is_first))
+        def _():
+            backs[0].wait_recv()
+
         for c in range(4):
             block = jnp.concatenate([ret_col[64 * c : 64 * c + 64, :].astype(F32)[0:60], head4(above, c)], axis=0)
             x_e[64 * c : 64 * c + 64, :] = block.astype(BF16)
@@ -588,25 +673,22 @@
     turn_biases()
     for _, c in z_sends[8:]:
         c.start()
-    relay_col()
-    main_ids(jnp.zeros((24, 128), F32), range(7))
     gather_main()
+    relay()
+    gather_last()
     qkv_main()
     spread((1, 2))
-    attention(0, 1)
     send_ids_done()
-    main_ids(reg_s[...].astype(F32), range(7, 8))
+    main_ids(reg_s[...].astype(F32), range(8))
     halo_ids()
+    attention(0, 2)
+    spread((3, 4))
     gather_halo()
     qkv_halo()
-    attention(2, 3)
-    spread((3, 4))
-    attention(3, 4)
+    attention(2, 4)
     share((1, 2))
     send_back_cols()
-    attention(1, 2)
     send_back_rows()
-    relay_back()
     share((3, 4))
     for c in loads[5:7]:
         c.wait()
@@ -616,6 +698,7 @@
     await_weights((3, 4))
     mlp_far(368, 400)
     mlp_far(768, 384)
+    far_windows()
     take_back()
     mlp_edge()
     finish()
@@ -628,7 +711,7 @@
     for group in range(1, 5):
         for c in xy_sends[group] + sib_sends[group]:
             c.wait_send()
-    for c in (send_cor, send_row, *send_ids, *backs[1:]):
+    for c in (send_cor, send_row, *send_ids, backs[2]):
         c.wait_send()
 
 
@@ -640,9 +723,9 @@
         vm((COLS, ROWS), jnp.int32),
         vm((1152, D), BF16),
         vm((1152, D), BF16),
-        vm((16 * WIN_PITCH, 3 * D), BF16),
-        vm((16 * WIN_PITCH, 128), BF16),
-        vm((16 * WIN_PITCH, D), F32),
+        vm((24 * WIN_PITCH, 3 * D), BF16),
+        vm((24 * WIN_PITCH, 128), BF16),
+        vm((24 * WIN_PITCH, D), F32),
         vm((D, 3 * D), BF16),
         vm((D, D), BF16),
         vm((8, 4, 2, 64, 256), BF16),
@@ -656,14 +739,21 @@
         vm((784, D), F32),
         vm((784, 2048), BF16),
         vm((16, D), BF16),
+        vm((32, D), BF16),
+        vm((5, ROWS, D), BF16),
+        vm((32, D), BF16),
+        vm((24, 128), jnp.int32),
+        vm((24, 128), jnp.int32),
         vm((16, D), BF16),
+        vm((256, D), BF16),
+        vm((576, D), BF16),
         vm((24, 128), jnp.int32),
         vm((24, 128), jnp.int32),
         vm((24, 128), jnp.int32),
         vm((24, 128), jnp.int32),
         vm((80, D), BF16),
         vm((4, ROWS, D), BF16),
-        vm((64, D), BF16),
+        vm((80, D), BF16),
         vm((16, D), BF16),
         vm((64, D), BF16),
         vm((16, D), BF16),
@@ -685,6 +775,8 @@
         dma((8,)),
         dma((17,)),
         dma((1,)),
+        dma((4,)),
+        dma((4,)),
     ]
     done = pl.pallas_call(
         kernel,

time: 62.4 us -> 70.9 us (1.14)
  the two profiles are of different devices: /device:TPU:32 before, /device:TPU:0 now
where the time goes in v5:
time: 70.9 us; the launch traced here: 70.7 us
  Pallas kernels  68.3 us (96%)
  local copies, waits for them, and re-layouts  2.39 us (3%)
    pallas_call x1, Pallas kernels, block(): pl.pallas_call(kernel, out_shape=jax.ShapeDtypeStruct((COLS, ROWS, D), BF...  68.3 us
    unnamed x1, local copies, waits for them, and re-layouts  2.39 us

profile of v5, /device:TPU:0, one launch (start us, length us, event | category | flops | bytes accessed | tf_op | source)
XLA Modules:
  0.0 70.7 jit_solution(670069769996992591)
XLA Ops:
  0.0 68.3 %shard_map.73 = bf16[18,64,512]{2,1,0:T(8,128)(2,1)} custom-call(bf16[18,64,512]{2,1,0:T(8,128)(2,1)} %bitcast.6, s32[18,64]{1,0:T(8,128)} %bitcast.9, bf16[512,1536]{1,0:T(8,128)(2,1)} %wqkv_h.1, bf16[512,512]{1,0:T(8,128)(2,1)} %wproj_h.1, bf16[4,2,64,256]{3,2,1,0:T(8,128)(2,1)} %bitcast.7, bf16[4,2,32,512]{3,2,1,0:T(8,128)(2,1)} %bitcast.8, ...), custom_call_target="tpu_custom_call" | custom-call | tf_op jit(solution)/shard_map/pallas_call | solution.py:781
  68.3 2.4 %copy.9 = bf16[64,18,512]{2,0,1:T(8,128)(2,1)} copy(bf16[64,18,512]{2,0,1:T(8,128)(2,1)} %bitcast.5) | data formatting | bytes 2359296

commit v6 on v5

--- a/solution.py
+++ b/solution.py
@@ -45,8 +45,8 @@
     braw, btmp, bias_v, bias_in, out_t, x_e, acc, hid, rel_in, rel_far,
     far_in, far_row, reg_f, reg_fs, far_cor, x_f, n_f,
     reg_out, reg_e, reg_s, reg_se, row_out, col_in, row_in, cor_in,
-    back_row, back_cor, ret_col, ret_row, ret_cor, out_v,
-    local_sem, out_sem, halo_send, halo_recv, ret_send, ret_recv, z_send, z_recv, xy_send, xy_recv,
+    back_row, back_cor, ret_col, ret_row, ret_cor,
+    local_sem, halo_send, halo_recv, ret_send, ret_recv, z_send, z_recv, xy_send, xy_recv,
     sib_send, sib_recv, rel_send, rel_recv, far_send, far_recv,
 ):
     lon = lax.axis_index("lon")
@@ -131,6 +131,22 @@
 
     more = jnp.where(jnp.logical_or(core == 0, far_relay), 1, 0)
     more = more + jnp.where(is_first, 15, 0) + jnp.where(is_last, 10, 0)
+    def turn_biases():
+        loads[2].wait()
+        braw[...] = jnp.zeros_like(braw)
+
+        def turn_bias(h, carry):
+            braw[:, 0:72] = bias_in[h]
+            first = [braw[pl.ds(c, 8, stride=9), :] for c in ORDER]
+            first.append(jnp.zeros((56, 128), F32))
+            btmp[...] = jnp.concatenate(first, axis=0).T
+            second = [btmp[pl.ds(c, 8, stride=9), :] for c in ORDER]
+            bias_v[pl.ds(pl.multiple_of(h * 72, 8), 72), :] = jnp.concatenate(second, axis=0) * LOG2E
+            return carry
+
+        lax.fori_loop(0, HEADS, turn_bias, 0)
+
+    turn_biases()
     pl.semaphore_wait(barrier, len(partners) + more)
 
     z_sends = []
@@ -307,21 +323,6 @@
         @pl.when(is_last)
         def _():
             far_sends[2].start()
-
-    def turn_biases():
-        loads[2].wait()
-        braw[...] = jnp.zeros_like(braw)
-
-        def turn_bias(h, carry):
-            braw[:, 0:72] = bias_in[h]
-            first = [braw[pl.ds(c, 8, stride=9), :] for c in ORDER]
-            first.append(jnp.zeros((56, 128), F32))
-            btmp[...] = jnp.concatenate(first, axis=0).T
-            second = [btmp[pl.ds(c, 8, stride=9), :] for c in ORDER]
-            bias_v[pl.ds(pl.multiple_of(h * 72, 8), 72), :] = jnp.concatenate(second, axis=0) * LOG2E
-            return carry
-
-        lax.fori_loop(0, HEADS, turn_bias, 0)
 
     lane24 = lax.broadcasted_iota(jnp.int32, (24, 128), 1)
     lane64 = lax.broadcasted_iota(jnp.int32, (64, 128), 1)
@@ -487,13 +488,36 @@
                 outs[8 * g + 4 + j] = res[32:64, 128:256] * sums[1]
         att[pl.ds(pl.multiple_of(w * WIN_PITCH, 16), 72), :] = jnp.concatenate(outs, axis=0).T[0:72]
 
-    def attend(i, carry):
-        for u in range(4):
-            window(jnp.where(i < 4, 8 * lax.rem(i, 2) + 2 * u + i // 2, 4 * i + u))
-        return carry
-
-    def attention(start, stop):
-        lax.fori_loop(start, stop, attend, 0)
+    def attention():
+        def attend(i, carry):
+            for u in range(4):
+                window(8 * lax.rem(i, 2) + 2 * u + i // 2)
+
+            @pl.when(i == 0)
+            def _():
+                spread((3, 4))
+
+            @pl.when(i == 1)
+            def _():
+                share((1, 2))
+                gather_halo()
+                qkv_halo()
+
+            @pl.when(i == 2)
+            def _():
+                share((3, 4))
+
+            return carry
+
+        lax.fori_loop(0, 4, attend, 0)
+
+    def far_attention():
+        def attend(i, carry):
+            for u in range(4):
+                window(4 * i + u)
+            return carry
+
+        lax.fori_loop(4, 6, attend, 0)
 
     def attended(w, pos):
         return att[w * WIN_PITCH + 8 * pos : w * WIN_PITCH + 8 * pos + 8, :]
@@ -596,7 +620,7 @@
             return carry
 
         lax.fori_loop(0, 6, step, 0)
-        attention(4, 6)
+        far_attention()
         order_halo(n_f, 2)
         mixed = x_f[...].astype(F32) + jnp.dot(n_f[0:256, :], wp_v[...], preferred_element_type=F32)
         ret_col[...] = mixed.astype(BF16)
@@ -617,13 +641,6 @@
         packed.append(jnp.zeros_like(packed[0]))
         back_row[...] = jnp.concatenate(packed, axis=0).astype(BF16)
         backs[2].start()
-
-    stores = []
-
-    def store_col(c):
-        found = pltpu.make_async_copy(out_v.at[c], out_h.at[c], out_sem.at[c])
-        found.start()
-        stores.append(found)
 
     def head4(packed, i):
         piece = packed[8 * (i // 2) : 8 * (i // 2) + 8]
@@ -651,45 +668,24 @@
             x_e[64 * c : 64 * c + 64, :] = block.astype(BF16)
             n_s[64 * c : 64 * c + 64, :] = norm(block)
 
-    def finish():
-        for c in range(4):
-            block = out_t[64 * c : 64 * c + 64, :].astype(F32)
-            out_v[c] = jnp.concatenate([block[60:64], block[0:60]], axis=0).astype(BF16)
-            store_col(c)
-        ends = out_t[LAST_AT:PAIR_AT, :].astype(F32)
-        for i, pair in enumerate(PAIRS):
-            block = out_t[PAIR_AT + 112 * i : PAIR_AT + 112 * i + 112, :].astype(F32)
-            for j, c in enumerate(pair):
-                k = LAST.index(c)
-                parts = [ends[8 * k + 4 : 8 * k + 8], block[56 * j : 56 * j + 56], ends[8 * k : 8 * k + 4]]
-                out_v[c + 4] = jnp.concatenate(parts, axis=0).astype(BF16)
-                store_col(c + 4)
-
     def send_ids_done():
         for c in send_ids:
             c.wait_recv()
 
     send_halos()
-    turn_biases()
+    gather_main()
     for _, c in z_sends[8:]:
         c.start()
-    gather_main()
-    relay()
     gather_last()
     qkv_main()
     spread((1, 2))
+    relay()
     send_ids_done()
     main_ids(reg_s[...].astype(F32), range(8))
     halo_ids()
-    attention(0, 2)
-    spread((3, 4))
-    gather_halo()
-    qkv_halo()
-    attention(2, 4)
-    share((1, 2))
+    attention()
     send_back_cols()
     send_back_rows()
-    share((3, 4))
     for c in loads[5:7]:
         c.wait()
     await_weights((1, 2))
@@ -698,11 +694,13 @@
     await_weights((3, 4))
     mlp_far(368, 400)
     mlp_far(768, 384)
+    stores = [local(out_t.at[pl.ds(PAIR_AT, 784), :], out_h.at[pl.ds(PAIR_AT, 784), :], 7)]
+    stores[0].start()
     far_windows()
     take_back()
     mlp_edge()
-    finish()
-
+    stores.append(local(out_t.at[pl.ds(0, PAIR_AT), :], out_h.at[pl.ds(0, PAIR_AT), :], 8))
+    stores[1].start()
     for c in stores:
         c.wait()
     relays_done()
@@ -713,6 +711,28 @@
             c.wait_send()
     for c in (send_cor, send_row, *send_ids, backs[2]):
         c.wait_send()
+
+
+def finish_kernel(tokens, out_h, out_v, sem):
+    stores = []
+
+    def store_col(c, parts):
+        out_v[c] = jnp.concatenate(parts, axis=0).astype(BF16)
+        found = pltpu.make_async_copy(out_v.at[c], out_h.at[c], sem.at[c])
+        found.start()
+        stores.append(found)
+
+    for c in range(4):
+        rows = tokens[64 * c : 64 * c + 64, :].astype(F32)
+        store_col(c, [rows[60:64], rows[0:60]])
+    ends = tokens[LAST_AT:PAIR_AT, :].astype(F32)
+    for i, pair in enumerate(PAIRS):
+        rows = tokens[PAIR_AT + 112 * i : PAIR_AT + 112 * i + 112, :].astype(F32)
+        for j, c in enumerate(pair):
+            k = LAST.index(c)
+            store_col(c + 4, [ends[8 * k + 4 : 8 * k + 8], rows[56 * j : 56 * j + 56], ends[8 * k : 8 * k + 4]])
+    for found in stores:
+        found.wait()
 
 
 def block(field, region, w_qkv, w_proj, w_up, w_down, position_bias):
@@ -760,9 +780,7 @@
         vm((256, D), BF16),
         vm((64, D), BF16),
         vm((16, D), BF16),
-        vm((COLS, ROWS, D), BF16),
-        dma((8,)),
-        dma((COLS,)),
+        dma((9,)),
         dma((6,)),
         dma((6,)),
         dma((3,)),
@@ -778,9 +796,9 @@
         dma((4,)),
         dma((4,)),
     ]
-    done = pl.pallas_call(
+    tokens = pl.pallas_call(
         kernel,
-        out_shape=jax.ShapeDtypeStruct((COLS, ROWS, D), BF16),
+        out_shape=jax.ShapeDtypeStruct((1152, D), BF16),
         in_specs=[pl.BlockSpec(memory_space=pl.ANY)] * 7,
         out_specs=pl.BlockSpec(memory_space=pl.ANY),
         scratch_shapes=scratch,
@@ -791,6 +809,14 @@
         field.transpose(1, 0, 2), region.T, w_qkv, w_proj,
         w_up.reshape(4, 2, 64, 256), w_down.reshape(4, 2, 32, D), position_bias,
     )
+    done = pl.pallas_call(
+        finish_kernel,
+        out_shape=jax.ShapeDtypeStruct((COLS, ROWS, D), BF16),
+        in_specs=[pl.BlockSpec(memory_space=pltpu.VMEM)],
+        out_specs=pl.BlockSpec(memory_space=pl.ANY),
+        scratch_shapes=[vm((COLS, ROWS, D), BF16), dma((COLS,))],
+        compiler_params=pltpu.CompilerParams(vmem_limit_bytes=16 * 1024 * 1024),
+    )(tokens)
     return done.transpose(1, 0, 2)
 
 

time: 70.9 us -> 72.9 us (1.028)
  Pallas kernels: 68.3 us -> 71.3 us
  local copies, waits for them, and re-layouts: 2.39 us -> 1.26 us
    pallas_call x1 -> x2, Pallas kernels: 68.3 us -> 71.3 us  [the longest x1 70.1 us: block(): pl.pallas_call(kernel, out_shape=jax.ShapeDtypeStruct((1152, D), BF16), i...]
    unnamed x1 -> x2, local copies, waits for them, and re-layouts: 2.39 us -> 1.26 us
where the time goes in v6:
time: 72.9 us; the launch traced here: 72.7 us
  Pallas kernels  71.3 us (98%)
  local copies, waits for them, and re-layouts  1.26 us (2%)
    pallas_call x1, Pallas kernels, block(): pl.pallas_call(kernel, out_shape=jax.ShapeDtypeStruct((1152, D), BF16), i...  70.1 us

profile of v6, /device:TPU:0, one launch (start us, length us, event | category | flops | bytes accessed | tf_op | source)
XLA Modules:
  0.0 72.7 jit_solution(11685035497117897241)
XLA Ops:
  0.0 70.1 %shard_map.73.tokens = bf16[1152,512]{1,0:T(8,128)(2,1)} custom-call(bf16[18,64,512]{2,1,0:T(8,128)(2,1)} %bitcast.5, s32[18,64]{1,0:T(8,128)} %bitcast.8, bf16[512,1536]{1,0:T(8,128)(2,1)} %wqkv_h.1, bf16[512,512]{1,0:T(8,128)(2,1)} %wproj_h.1, bf16[4,2,64,256]{3,2,1,0:T(8,128)(2,1)} %bitcast.6, bf16[4,2,32,512]{3,2,1,0:T(8,128)(2,1)} %bitcast.7, ...), custom_call_target="tpu_custom_call" | custom-call | tf_op jit(solution)/shard_map/pallas_call | solution.py:799
  70.1 0.0 copy-start
  70.1 1.3 %copy-done = bf16[1152,512]{1,0:T(8,128)(2,1)S(1)} copy-done((bf16[1152,512]{1,0:T(8,128)(2,1)S(1)}, bf16[1152,512]{1,0:T(8,128)(2,1)}, u32[]{:S(2)}) %copy-start) | copy-done | bytes 1179672
  71.4 1.2 %shard_map.74 = bf16[18,64,512]{2,1,0:T(8,128)(2,1)} custom-call(bf16[1152,512]{1,0:T(8,128)(2,1)S(1)} %copy-done), custom_call_target="tpu_custom_call" | custom-call | tf_op jit(solution)/shard_map/pallas_call | solution.py:812
Async XLA Ops:
  70.1 1.3 %copy-start = (bf16[1152,512]{1,0:T(8,128)(2,1)S(1)}, bf16[1152,512]{1,0:T(8,128)(2,1)}, u32[]{:S(2)}) copy-start(bf16[1152,512]{1,0:T(8,128)(2,1)} %shard_map.73.tokens) | copy-start | bytes 3538948

commit v7 on v6

--- a/solution.py
+++ b/solution.py
@@ -299,8 +299,6 @@
 
     def send_halos():
         start_col()
-        for _, c in z_sends[0:8]:
-            c.start()
         loads[1].wait()
         reg_out[...] = jnp.zeros_like(reg_out)
         reg_out[0:18, 0:64] = region_v[...]
@@ -323,6 +321,9 @@
         @pl.when(is_last)
         def _():
             far_sends[2].start()
+
+        for _, c in z_sends[0:8]:
+            c.start()
 
     lane24 = lax.broadcasted_iota(jnp.int32, (24, 128), 1)
     lane64 = lax.broadcasted_iota(jnp.int32, (64, 128), 1)
@@ -413,10 +414,17 @@
 
         def step(n, carry):
             lanes = pl.ds(pl.multiple_of(n * 256, 256), 256)
-            res = jnp.dot(n_s[pl.ds(LAST_AT, 896), :], wq_v[:, lanes], preferred_element_type=F32)
+            res = jnp.dot(n_s[pl.ds(PAIR_AT, 784), :], wq_v[:, lanes], preferred_element_type=F32)
             for i in range(7):
-                scatter(lanes, i, res[PAIR_ROWS * (i + 1) : PAIR_ROWS * (i + 2)])
-            last = res[0:PAIR_ROWS]
+                scatter(lanes, i, res[PAIR_ROWS * i : PAIR_ROWS * (i + 1)])
+            return carry
+
+        lax.fori_loop(0, 6, step, 0)
+
+    def qkv_last():
+        def step(n, carry):
+            lanes = pl.ds(pl.multiple_of(n * 256, 256), 256)
+            last = jnp.dot(n_s[pl.ds(LAST_AT, PAIR_ROWS), :], wq_v[:, lanes], preferred_element_type=F32)
             fill = jnp.zeros((8, 256), F32)
             qw[pl.ds(14 * WIN_PITCH, 80), lanes] = jnp.concatenate([last[0:72], fill], axis=0).astype(BF16)
             qw[pl.ds(15 * WIN_PITCH + 32, 48), lanes] = jnp.concatenate([last[72:112], fill], axis=0).astype(BF16)
@@ -496,6 +504,8 @@
             @pl.when(i == 0)
             def _():
                 spread((3, 4))
+                gather_last()
+                qkv_last()
 
             @pl.when(i == 1)
             def _():
@@ -584,7 +594,6 @@
         return jnp.concatenate(packed, axis=0).astype(BF16)
 
     def send_back_cols():
-        loads[4].wait()
         order_halo(n_s, 1)
         project(0, 256)
         back_cor[...] = pack_ends(x_s)
@@ -676,7 +685,6 @@
     gather_main()
     for _, c in z_sends[8:]:
         c.start()
-    gather_last()
     qkv_main()
     spread((1, 2))
     relay()
@@ -684,8 +692,10 @@
     main_ids(reg_s[...].astype(F32), range(8))
     halo_ids()
     attention()
+    loads[4].wait()
+    send_back_rows()
     send_back_cols()
-    send_back_rows()
+    far_windows()
     for c in loads[5:7]:
         c.wait()
     await_weights((1, 2))
@@ -696,7 +706,6 @@
     mlp_far(768, 384)
     stores = [local(out_t.at[pl.ds(PAIR_AT, 784), :], out_h.at[pl.ds(PAIR_AT, 784), :], 7)]
     stores[0].start()
-    far_windows()
     take_back()
     mlp_edge()
     stores.append(local(out_t.at[pl.ds(0, PAIR_AT), :], out_h.at[pl.ds(0, PAIR_AT), :], 8))

time: 72.9 us -> 64.3 us (0.88)
  the two profiles are of different devices: /device:TPU:0 before, /device:TPU:32 now
where the time goes in v7:
time: 64.3 us; the launch traced here: 64.2 us
  Pallas kernels  62.8 us (98%)
  local copies, waits for them, and re-layouts  1.26 us (2%)
    pallas_call x1, Pallas kernels, block(): pl.pallas_call(kernel, out_shape=jax.ShapeDtypeStruct((1152, D), BF16), i...  61.6 us

profile of v7, /device:TPU:32, one launch (start us, length us, event | category | flops | bytes accessed | tf_op | source)
XLA Modules:
  0.0 64.2 jit_solution(5894572915114136865)
XLA Ops:
  0.0 61.6 %shard_map.73.tokens = bf16[1152,512]{1,0:T(8,128)(2,1)} custom-call(bf16[18,64,512]{2,1,0:T(8,128)(2,1)} %bitcast.5, s32[18,64]{1,0:T(8,128)} %bitcast.8, bf16[512,1536]{1,0:T(8,128)(2,1)} %wqkv_h.1, bf16[512,512]{1,0:T(8,128)(2,1)} %wproj_h.1, bf16[4,2,64,256]{3,2,1,0:T(8,128)(2,1)} %bitcast.6, bf16[4,2,32,512]{3,2,1,0:T(8,128)(2,1)} %bitcast.7, ...), custom_call_target="tpu_custom_call" | custom-call | tf_op jit(solution)/shard_map/pallas_call | solution.py:808
  61.6 0.0 copy-start
  61.6 1.3 %copy-done = bf16[1152,512]{1,0:T(8,128)(2,1)S(1)} copy-done((bf16[1152,512]{1,0:T(8,128)(2,1)S(1)}, bf16[1152,512]{1,0:T(8,128)(2,1)}, u32[]{:S(2)}) %copy-start) | copy-done | bytes 1179672
  62.9 1.2 %shard_map.74 = bf16[18,64,512]{2,1,0:T(8,128)(2,1)} custom-call(bf16[1152,512]{1,0:T(8,128)(2,1)S(1)} %copy-done), custom_call_target="tpu_custom_call" | custom-call | tf_op jit(solution)/shard_map/pallas_call | solution.py:821
Async XLA Ops:
  61.6 1.3 %copy-start = (bf16[1152,512]{1,0:T(8,128)(2,1)S(1)}, bf16[1152,512]{1,0:T(8,128)(2,1)}, u32[]{:S(2)}) copy-start(bf16[1152,512]{1,0:T(8,128)(2,1)} %shard_map.73.tokens) | copy-start | bytes 3538948

commit v8 on v7

--- a/solution.py
+++ b/solution.py
@@ -147,7 +147,6 @@
         lax.fori_loop(0, HEADS, turn_bias, 0)
 
     turn_biases()
-    pl.semaphore_wait(barrier, len(partners) + more)
 
     z_sends = []
     for i, dev in enumerate(z_to):
@@ -298,10 +297,8 @@
     scale = LOG2E * 32 ** (-0.5)
 
     def send_halos():
+        pl.semaphore_wait(barrier, len(partners) + more)
         start_col()
-        loads[1].wait()
-        reg_out[...] = jnp.zeros_like(reg_out)
-        reg_out[0:18, 0:64] = region_v[...]
         for c in send_ids:
             c.start()
 
@@ -310,7 +307,6 @@
             for c in far_sends[0:2]:
                 c.start()
 
-        loads[0].wait()
         tops = [field_v[c, 0:16, :].astype(F32)[0:8] for c in range(COLS)]
         packed = [jnp.where(sub8 < 4, tops[2 * i], swap4(tops[2 * i + 1])) for i in range(9)]
         packed.append(jnp.zeros_like(packed[0]))
@@ -410,8 +406,6 @@
         n_s[at, :] = norm(block)
 
     def qkv_main():
-        loads[3].wait()
-
         def step(n, carry):
             lanes = pl.ds(pl.multiple_of(n * 256, 256), 256)
             res = jnp.dot(n_s[pl.ds(PAIR_AT, 784), :], wq_v[:, lanes], preferred_element_type=F32)
@@ -681,11 +675,32 @@
         for c in send_ids:
             c.wait_recv()
 
-    send_halos()
-    gather_main()
-    for _, c in z_sends[8:]:
-        c.start()
-    qkv_main()
+    early = jnp.logical_or(is_first, jnp.logical_and(z_hi == 0, lat < 5))
+    turn = jnp.where(early, 0, 1)
+    loads[1].wait()
+    reg_out[...] = jnp.zeros_like(reg_out)
+    reg_out[0:18, 0:64] = region_v[...]
+    loads[0].wait()
+    loads[3].wait()
+
+    def opening(k, carry):
+        @pl.when(k == 1 - turn)
+        def _():
+            send_halos()
+
+        @pl.when(k == 1)
+        def _():
+            for _, c in z_sends[8:]:
+                c.start()
+
+        @pl.when(k == turn)
+        def _():
+            gather_main()
+            qkv_main()
+
+        return carry
+
+    lax.fori_loop(0, 2, opening, 0)
     spread((1, 2))
     relay()
     send_ids_done()
@@ -695,12 +710,12 @@
     loads[4].wait()
     send_back_rows()
     send_back_cols()
-    far_windows()
     for c in loads[5:7]:
         c.wait()
     await_weights((1, 2))
     mlp_near(368, 400)
     mlp_near(768, 384)
+    far_windows()
     await_weights((3, 4))
     mlp_far(368, 400)
     mlp_far(768, 384)

time: 64.3 us -> 64.3 us (level)
  no operation moved by 1% of the time
where the time goes in v8:
time: 64.3 us; the launch traced here: 64.2 us
  Pallas kernels  62.7 us (98%)
  local copies, waits for them, and re-layouts  1.26 us (2%)
    pallas_call x1, Pallas kernels, block(): pl.pallas_call(kernel, out_shape=jax.ShapeDtypeStruct((1152, D), BF16), i...  61.6 us

profile of v8, /device:TPU:32, one launch (start us, length us, event | category | flops | bytes accessed | tf_op | source)
XLA Modules:
  0.0 64.2 jit_solution(16312111159027740442)
XLA Ops:
  0.0 61.6 %shard_map.73.tokens = bf16[1152,512]{1,0:T(8,128)(2,1)} custom-call(bf16[18,64,512]{2,1,0:T(8,128)(2,1)} %bitcast.5, s32[18,64]{1,0:T(8,128)} %bitcast.8, bf16[512,1536]{1,0:T(8,128)(2,1)} %wqkv_h.1, bf16[512,512]{1,0:T(8,128)(2,1)} %wproj_h.1, bf16[4,2,64,256]{3,2,1,0:T(8,128)(2,1)} %bitcast.6, bf16[4,2,32,512]{3,2,1,0:T(8,128)(2,1)} %bitcast.7, ...), custom_call_target="tpu_custom_call" | custom-call | tf_op jit(solution)/shard_map/pallas_call | solution.py:823
  61.6 0.0 copy-start
  61.6 1.3 %copy-done = bf16[1152,512]{1,0:T(8,128)(2,1)S(1)} copy-done((bf16[1152,512]{1,0:T(8,128)(2,1)S(1)}, bf16[1152,512]{1,0:T(8,128)(2,1)}, u32[]{:S(2)}) %copy-start) | copy-done | bytes 1179672
  62.8 1.2 %shard_map.74 = bf16[18,64,512]{2,1,0:T(8,128)(2,1)} custom-call(bf16[1152,512]{1,0:T(8,128)(2,1)S(1)} %copy-done), custom_call_target="tpu_custom_call" | custom-call | tf_op jit(solution)/shard_map/pallas_call | solution.py:836
Async XLA Ops:
  61.6 1.3 %copy-start = (bf16[1152,512]{1,0:T(8,128)(2,1)S(1)}, bf16[1152,512]{1,0:T(8,128)(2,1)}, u32[]{:S(2)}) copy-start(bf16[1152,512]{1,0:T(8,128)(2,1)} %shard_map.73.tokens) | copy-start | bytes 3538948
